TPU v7x, 32 devices: a whole 2x2x4 slice. The times are simulated.
32 devices in a mesh: cells: 16 (over z, y, x), rep: 2 (over core).
Axes of the slice: x: 2, y: 2, z: 4, core: 2. Of those that a mesh axis runs over, the one named last changes fastest.
Arguments:
- cells_x: bfloat16 [18432, 7000], P(('cells', 'rep')), may hold values from -12 to 12
- latent_noise: float32 [18432, 100], P(('cells', 'rep')), may hold values from -6 to 6
- group_ids: int32 [18432], P(('cells', 'rep')), may hold values from 0 to 63, as said below
- owner_table: int32 [16, 4], replicated, may hold values from 0 to 31, as said below
- owner_mask: int32 [16, 4], replicated, may hold values from 0 to 1
- enc_w1: bfloat16 [7000, 800], replicated, may hold values from -0.0625 to 0.0625
- enc_w2: bfloat16 [800, 800], replicated, may hold values from -0.21875 to 0.21875
- head_w: bfloat16 [800, 200], replicated, may hold values from -0.21875 to 0.21875
- head_b: float32 [200], replicated, may hold values from -3 to 3
- dec_w1: bfloat16 [100, 800], replicated, may hold values from -0.625 to 0.625
- dec_w2: bfloat16 [800, 800], replicated, may hold values from -0.21875 to 0.21875
- out_w: bfloat16 [800, 7000], replicated, may hold values from -0.109375 to 0.109375
- out_b: float32 [7000], replicated, may hold values from -0.05 to 0.05
- bn_gain: float32 [4, 800], replicated, may hold values from 0.25 to 1.75
- bn_shift: float32 [4, 800], replicated, may hold values from -0.7 to -0.3
Outputs:
- grad_x: float32 [18432, 7000], P(('cells', 'rep'))
- grad_enc_w1: float32 [6400, 875], P(('cells', 'rep'))
- grad_narrow: float32 [2048, 625], P(('cells', 'rep'))
- grad_head_w: float32 [800, 200], replicated
- grad_dec_w1: float32 [100, 800], replicated
- grad_head_b: float32 [200], replicated
- grad_out_w: float32 [6400, 875], P(('cells', 'rep'))
- grad_out_b: float32 [7000], replicated
- grad_gain: float32 [4, 800], replicated
- grad_shift: float32 [4, 800], replicated
- offsets: float32 [16, 4, 100], P('cells')
Inputs may be any that keep to these rules, and one draw needn't show every extreme that they name: `group_ids`: A cell's group is 2 * its population + its condition (1 stimulated, 0 control); populations differ in size, and some groups hold no cells. `owner_table`: each population 0 to 31 stands in exactly one live slot; a row's live slots come first and masked slots hold 0; some rows have all 4 slots live and some none.
All inputs are finite; a program needn't handle non-finite values.
Results may differ from a plain program's by a relative error of at most 0.018.
Values sent between devices are 32-bit elements; how exact they have to be, the bound alone decides.
A program may use at most 256 MiB of HBM per device.

v0:
```python
import jax
import jax.numpy as jnp
from jax import lax
from jax.sharding import PartitionSpec as P

POP_DEV = 2
FLAT_COLS = 875
NARROW_COLS = 625
FLAT_ROWS = 6400
NARROW_ROWS = 2048


NORM_EPSILON = 1e-05
KL_WEIGHT = 5e-05
OFFSET_WEIGHT = 200.0


def contract_rows(left, right):
    return lax.dot_general(
        left, right, (((0,), (0,)), ((), ())), preferred_element_type=jnp.float32
    )


def contract_cols(left, right):
    return lax.dot_general(
        left, right, (((1,), (1,)), ((), ())), preferred_element_type=jnp.float32
    )


def exact_rows(left, right):
    return lax.dot_general(
        left,
        right,
        (((0,), (0,)), ((), ())),
        precision=lax.Precision.HIGHEST,
        preferred_element_type=jnp.float32,
    )


def exact_product(left, right):
    return jnp.dot(left, right, precision=lax.Precision.HIGHEST, preferred_element_type=jnp.float32)


def norm_forward(values, norm_gain, norm_shift, cell_total):
    column_sum = lax.psum(jnp.sum(values, axis=0), ("cells", "rep"))
    centered = values - column_sum / cell_total
    square_sum = lax.psum(jnp.sum(centered * centered, axis=0), ("cells", "rep"))
    spread = square_sum / cell_total
    inv_std = lax.rsqrt(spread + NORM_EPSILON)
    normed = centered * inv_std
    pre_act = norm_gain * normed + norm_shift
    active = (pre_act * jax.nn.sigmoid(pre_act)).astype(jnp.bfloat16)
    return (active, (normed, pre_act, inv_std))


def norm_backward(grad_act, saved_norm, norm_gain, cell_total):
    normed, pre_act, inv_std = saved_norm
    gate_value = jax.nn.sigmoid(pre_act)
    grad_pre = grad_act * gate_value * (1.0 + pre_act * (1.0 - gate_value))
    grad_shift, grad_gain = lax.psum(
        (jnp.sum(grad_pre, axis=0), jnp.sum(grad_pre * normed, axis=0)), ("cells", "rep")
    )
    grad_in = (
        norm_gain
        * inv_std
        * (grad_pre - grad_shift / cell_total - normed * (grad_gain / cell_total))
    )
    return (grad_in.astype(jnp.bfloat16), grad_gain, grad_shift)


def group_terms(latent_mean, group_ids, owner_table, owner_mask, populations):
    groups = 2 * populations
    latent_width = latent_mean.shape[1]
    owners = owner_table.shape[0]
    slot_count = owner_table.shape[1]
    member = (group_ids[:, None] == jnp.arange(groups, dtype=jnp.int32)[None, :]).astype(
        jnp.float32
    )
    local_sums = exact_rows(member, latent_mean)
    local_count = jnp.sum(member, axis=0)
    select = (
        (owner_table[:, :, None] == jnp.arange(populations, dtype=jnp.int32)[None, None, :])
        * owner_mask[:, :, None]
    ).astype(jnp.float32)
    select = select.reshape(owners * slot_count, populations)
    my_row = lax.axis_index("cells")
    pair_sums, pair_count = lax.psum((local_sums, local_count), "rep")
    by_pop = pair_sums.reshape(populations, 2 * latent_width)
    count_pop = pair_count.reshape(populations, 2)
    outgoing = exact_product(select, by_pop).reshape(owners, slot_count, 2 * latent_width)
    out_count = exact_product(select, count_pop).reshape(owners, slot_count, 2)
    arrived, arrived_count = (
        lax.all_to_all(outgoing, "cells", split_axis=0, concat_axis=0, tiled=True),
        lax.all_to_all(out_count, "cells", split_axis=0, concat_axis=0, tiled=True),
    )
    totals = jnp.sum(arrived, axis=0).reshape(slot_count, 2, latent_width)
    counted = jnp.maximum(jnp.sum(arrived_count, axis=0), 1.0)
    group_means = totals / counted[:, :, None]
    offset = group_means[:, 1] - group_means[:, 0]
    offset_sum = lax.psum(jnp.sum(offset, axis=0), "cells")
    my_mask = lax.dynamic_slice_in_dim(owner_mask, my_row, 1, 0)[0].astype(jnp.float32)
    grad_offset = (
        2.0 * OFFSET_WEIGHT / populations * (offset - offset_sum / populations) * my_mask[:, None]
    )
    grad_means = jnp.stack([-grad_offset, grad_offset], axis=1) / counted[:, :, None]
    returned = lax.all_gather(
        grad_means.reshape(1, slot_count, 2 * latent_width), "cells", axis=0, tiled=True
    )
    grad_pop = exact_rows(select, returned.reshape(owners * slot_count, 2 * latent_width))
    offsets = offset[None]
    grad_group = exact_product(member, grad_pop.reshape(groups, latent_width))
    return (grad_group, offsets)


def shards(
    cells_x,
    latent_noise,
    group_ids,
    owner_table,
    owner_mask,
    enc_w1,
    enc_w2,
    head_w,
    head_b,
    dec_w1,
    dec_w2,
    out_w,
    out_b,
    bn_gain,
    bn_shift,
):
    cell_total = float(cells_x.shape[0] * lax.axis_size("cells") * lax.axis_size("rep"))
    populations = POP_DEV * lax.axis_size("cells")
    latent_width = dec_w1.shape[0]
    gene_count = cells_x.shape[1]
    first_pre = jnp.dot(cells_x, enc_w1, preferred_element_type=jnp.float32)
    first_act, first_kept = norm_forward(first_pre, bn_gain[0], bn_shift[0], cell_total)
    second_pre = jnp.dot(first_act, enc_w2, preferred_element_type=jnp.float32)
    second_act, second_kept = norm_forward(second_pre, bn_gain[1], bn_shift[1], cell_total)
    head_out = jnp.dot(second_act, head_w, preferred_element_type=jnp.float32) + head_b
    latent_mean = head_out[:, :latent_width]
    logvar = head_out[:, latent_width:]
    deviation = jnp.exp(0.5 * logvar)
    latent_draw = (latent_mean + deviation * latent_noise).astype(jnp.bfloat16)
    grad_group, offsets = group_terms(latent_mean, group_ids, owner_table, owner_mask, populations)
    third_pre = jnp.dot(latent_draw, dec_w1, preferred_element_type=jnp.float32)
    third_act, third_kept = norm_forward(third_pre, bn_gain[2], bn_shift[2], cell_total)
    fourth_pre = jnp.dot(third_act, dec_w2, preferred_element_type=jnp.float32)
    fourth_act, fourth_kept = norm_forward(fourth_pre, bn_gain[3], bn_shift[3], cell_total)
    residual = (
        jnp.dot(fourth_act, out_w, preferred_element_type=jnp.float32)
        + out_b
        - cells_x.astype(jnp.float32)
    )
    grad_recon = (residual * (2.0 / cell_total)).astype(jnp.bfloat16)
    grad_out_w = contract_rows(fourth_act, grad_recon)
    grad_out_b = jnp.sum(grad_recon.astype(jnp.float32), axis=0)
    grad_fourth = contract_cols(grad_recon, out_w)
    grad_pre4, gain_three, shift_three = norm_backward(
        grad_fourth, fourth_kept, bn_gain[3], cell_total
    )
    grad_dec_w2 = contract_rows(third_act, grad_pre4)
    grad_third = contract_cols(grad_pre4, dec_w2)
    grad_pre3, gain_two, shift_two = norm_backward(grad_third, third_kept, bn_gain[2], cell_total)
    grad_dec_w1 = contract_rows(latent_draw, grad_pre3)
    grad_latent = contract_cols(grad_pre3, dec_w1)
    kl_scale = KL_WEIGHT * gene_count / cell_total
    grad_mean = grad_latent + kl_scale * latent_mean + grad_group
    grad_logvar = grad_latent * latent_noise * (0.5 * deviation) + 0.5 * kl_scale * (
        jnp.exp(logvar) - 1.0
    )
    grad_head = jnp.concatenate([grad_mean, grad_logvar], axis=1).astype(jnp.bfloat16)
    grad_head_w = contract_rows(second_act, grad_head)
    grad_head_b = jnp.sum(grad_head.astype(jnp.float32), axis=0)
    grad_second = contract_cols(grad_head, head_w)
    grad_pre2, gain_one, shift_one = norm_backward(grad_second, second_kept, bn_gain[1], cell_total)
    grad_enc_w2 = contract_rows(first_act, grad_pre2)
    grad_first = contract_cols(grad_pre2, enc_w2)
    grad_pre1, gain_zero, shift_zero = norm_backward(grad_first, first_kept, bn_gain[0], cell_total)
    grad_enc_w1 = contract_rows(cells_x, grad_pre1)
    grad_x = cell_total * contract_cols(grad_pre1, enc_w1) - 2.0 * residual
    summed_head_b, summed_out_b, summed_head_w, summed_dec_w1 = lax.psum(
        (grad_head_b, grad_out_b, grad_head_w, grad_dec_w1), ("cells", "rep")
    )
    flat_out = grad_out_w.reshape(FLAT_ROWS, FLAT_COLS)
    flat_enc = grad_enc_w1.reshape(FLAT_ROWS, FLAT_COLS)
    flat_narrow = jnp.concatenate([grad_enc_w2.reshape(-1), grad_dec_w2.reshape(-1)]).reshape(
        NARROW_ROWS, NARROW_COLS
    )
    shard_out, shard_enc, shard_narrow = (
        lax.psum_scatter(flat_out, ("cells", "rep"), scatter_dimension=0, tiled=True),
        lax.psum_scatter(flat_enc, ("cells", "rep"), scatter_dimension=0, tiled=True),
        lax.psum_scatter(flat_narrow, ("cells", "rep"), scatter_dimension=0, tiled=True),
    )
    grad_gain = jnp.stack([gain_zero, gain_one, gain_two, gain_three])
    grad_shift = jnp.stack([shift_zero, shift_one, shift_two, shift_three])
    return (
        grad_x,
        shard_enc,
        shard_narrow,
        summed_head_w,
        summed_dec_w1,
        summed_head_b,
        shard_out,
        summed_out_b,
        grad_gain,
        grad_shift,
        offsets,
    )


def solution(mesh):
    return jax.shard_map(
        shards,
        mesh=mesh,
        in_specs=(
            P(("cells", "rep"), None),
            P(("cells", "rep"), None),
            P(("cells", "rep")),
            P(),
            P(),
            P(),
            P(),
            P(),
            P(),
            P(),
            P(),
            P(),
            P(),
            P(),
            P(),
        ),
        out_specs=(
            P(("cells", "rep"), None),
            P(("cells", "rep"), None),
            P(("cells", "rep"), None),
            P(),
            P(),
            P(),
            P(("cells", "rep"), None),
            P(),
            P(),
            P(),
            P("cells", None, None),
        ),
        check_vma=False,
    )
```

profile of v0, /device:TPU:0, one launch (start us, length us, event | category | flops | bytes accessed | tf_op | source)
XLA Modules:
  0.0 1445.9 jit_solution(3137700688648134539)
XLA Ops:
  7.2 0.9 convert_reduce_fusion.2
  8.3 1.5 slice_reduce_fusion.2
  9.8 1.5 slice_reduce_fusion
  11.3 13.4 fusion.44
  24.7 42.0 %psum.161 = f32[800]{0:T(1024)S(1)} all-reduce(f32[800]{0:T(1024)S(1)} %get-tuple-element.53), channel_id=1, replica_groups=mesh['cells'=16,'rep'=2] {'cells','rep'}, use_global_device_ids=true, to_apply=%region_1.0 | all-reduce | flops 800 | bytes 6400 | tf_op jit(solution)/shard_map/psum | solution.py:45
  67.2 40.1 %psum.162 = f32[800]{0:T(1024)S(1)} all-reduce(f32[800]{0:T(1024)S(1)} %multiply_reduce_fusion.7), channel_id=1, replica_groups=mesh['cells'=16,'rep'=2] {'cells','rep'}, use_global_device_ids=true, to_apply=%region_3.0 | all-reduce | flops 800 | bytes 6400 | tf_op jit(solution)/shard_map/psum | solution.py:47
  107.3 1.0 multiply_convert_fusion.8
  108.6 2.8 fusion.45
  111.4 40.0 %psum.163 = f32[800]{0:T(1024)S(1)} all-reduce(f32[800]{0:T(1024)S(1)} %get-tuple-element.55), channel_id=1, replica_groups=mesh['cells'=16,'rep'=2] {'cells','rep'}, use_global_device_ids=true, to_apply=%region_5.0 | all-reduce | flops 800 | bytes 6400 | tf_op jit(solution)/shard_map/psum | solution.py:45
  151.5 2.0 multiply_reduce_fusion.6
  153.5 40.1 %psum.164 = f32[800]{0:T(1024)S(1)} all-reduce(f32[800]{0:T(1024)S(1)} %multiply_reduce_fusion.6), channel_id=1, replica_groups=mesh['cells'=16,'rep'=2] {'cells','rep'}, use_global_device_ids=true, to_apply=%region_7.0 | all-reduce | flops 800 | bytes 6400 | tf_op jit(solution)/shard_map/psum | solution.py:47
  194.2 1.0 multiply_convert_fusion.7
  195.2 1.0 copy-done.6
  197.1 4.0 all-reduce.7
  202.2 6.4 all-to-all-start.1
  209.4 1.5 fusion.46
  210.9 40.9 %psum.165 = f32[800]{0:T(1024)S(1)} all-reduce(f32[800]{0:T(1024)S(1)} %get-tuple-element.57), channel_id=1, replica_groups=mesh['cells'=16,'rep'=2] {'cells','rep'}, use_global_device_ids=true, to_apply=%region_9.0 | all-reduce | flops 800 | bytes 6400 | tf_op jit(solution)/shard_map/psum | solution.py:45
  252.2 40.1 %psum.166 = f32[800]{0:T(1024)} all-reduce(f32[800]{0:T(1024)S(1)} %multiply_reduce_fusion.5), channel_id=1, replica_groups=mesh['cells'=16,'rep'=2] {'cells','rep'}, use_global_device_ids=true, to_apply=%region_11.0 | all-reduce | flops 800 | bytes 6400 | tf_op jit(solution)/shard_map/psum | solution.py:47
  292.3 1.3 fusion.35
  293.6 1.0 multiply_convert_fusion.6
  294.6 2.8 fusion.47
  297.4 40.3 %psum.167 = f32[800]{0:T(1024)} all-reduce(f32[800]{0:T(1024)S(1)} %get-tuple-element.59), channel_id=1, replica_groups=mesh['cells'=16,'rep'=2] {'cells','rep'}, use_global_device_ids=true, to_apply=%region_13.0 | all-reduce | flops 800 | bytes 6400 | tf_op jit(solution)/shard_map/psum | solution.py:45
  338.4 2.6 multiply_reduce_fusion.4
  341.0 40.5 %psum.168 = f32[800]{0:T(1024)} all-reduce(f32[800]{0:T(1024)} %multiply_reduce_fusion.4), channel_id=1, replica_groups=mesh['cells'=16,'rep'=2] {'cells','rep'}, use_global_device_ids=true, to_apply=%region_15.0 | all-reduce | flops 800 | bytes 6400 | tf_op jit(solution)/shard_map/psum | solution.py:47
  381.5 1.3 fusion.36
  382.9 19.8 %convert_reduce_fusion = (f32[7000]{0:T(1024)}, f32[576,7000]{1,0:T(8,128)}) fusion(bf16[576,7000]{1,0:T(8,128)(2,1)} %param.15, f32[7000]{0:T(1024)} %param.27, bf16[800,7000]{1,0:T(8,128)(2,1)} %param.26, f32[576,800]{0,1:T(8,128)} %get-tuple-element.60, f32[800]{0:T(1024)} %get-tuple-element.23, f32[800]{0:T(1024)S(1)} %get-tuple-element.52, ...), kind=kOutput, calls=%fused_computation | convolution fusion | flops 6483564032 | bytes 37304000 | tf_op jit(solution)/shard_map/dot_general | solution.py:151
  402.7 20.0 %fusion.41 = (f32[800]{0:T(1024)}, f32[800]{0:T(1024)}, f32[576,800]{0,1:T(8,128)}) fusion(f32[800]{0:T(1024)S(1)} %get-tuple-element.52, f32[576,800]{0,1:T(8,128)S(1)} %copy-done.8, f32[800]{0:T(1024)S(1)} %broadcast_multiply_fusion.8, f32[800]{0:T(1024)S(1)} %copy-done.36, f32[800]{0:T(1024)S(1)} %copy-done.28, bf16[800,7000]{1,0:T(8,128)(2,1)} %param.26, ...), kind=kOutput, calls=%fused_computation.124 | convolution fusion | flops 6466173952 | bytes 31033600 | tf_op jit(solution)/shard_map/dot_general | solution.py:25
  422.6 40.7 %all-reduce.5 = (f32[800]{0:T(1024)}, f32[800]{0:T(1024)}) all-reduce(f32[800]{0:T(1024)} %get-tuple-element.18, f32[800]{0:T(1024)} %get-tuple-element.17), channel_id=1, replica_groups=mesh['cells'=16,'rep'=2] {'cells','rep'}, use_global_device_ids=true, to_apply=%region_19.0 | all-reduce | flops 1600 | bytes 12800 | tf_op jit(solution)/shard_map/psum | solution.py:60
  464.0 2.8 multiply_convert_fusion.4
  466.8 3.0 fusion.49
  469.8 3.7 fusion.40
  473.5 40.8 %all-reduce.4 = (f32[800]{0:T(1024)S(1)}, f32[800]{0:T(1024)S(1)}) all-reduce(f32[800]{0:T(1024)} %get-tuple-element.16, f32[800]{0:T(1024)} %get-tuple-element.15), channel_id=1, replica_groups=mesh['cells'=16,'rep'=2] {'cells','rep'}, use_global_device_ids=true, to_apply=%region_23.0 | all-reduce | flops 1600 | bytes 12800 | tf_op jit(solution)/shard_map/psum | solution.py:60
  514.3 2.3 multiply_convert_fusion.3
  516.7 1.2 fusion.50
  517.9 1.1 add_convert_fusion
  519.9 5.9 concatenate.14
  526.0 6.5 all-to-all-start
  532.8 7.4 all-to-all-done
  540.4 37.5 %psum.175 = f32[100]{0:T(128)S(1)} all-reduce(f32[100]{0:T(128)S(1)} %get-tuple-element.43), channel_id=1, replica_groups=mesh['cells'=16,'rep'=2] {'cells'}, use_global_device_ids=true, to_apply=%region_30.0 | all-reduce | flops 100 | bytes 800 | tf_op jit(solution)/shard_map/psum | solution.py:100
  578.1 36.8 %all_gather.3 = f32[16,4,200]{2,1,0:T(4,128)S(1)} all-gather(f32[1,4,200]{2,1,0:T(4,128)S(1)} %div.115), channel_id=1, replica_groups=mesh['cells'=16,'rep'=2] {'cells'}, dimensions={0}, use_global_device_ids=true | all-gather | bytes 54400 | tf_op jit(solution)/shard_map/all_gather | solution.py:106
  615.3 1.4 fusion
  616.7 1.5 fusion.6
  618.2 3.7 fusion.39
  621.9 37.0 %all-reduce.3 = (f32[800]{0:T(1024)S(1)}, f32[800]{0:T(1024)S(1)}) all-reduce(f32[800]{0:T(1024)S(1)} %get-tuple-element.14, f32[800]{0:T(1024)S(1)} %get-tuple-element.13), channel_id=1, replica_groups=mesh['cells'=16,'rep'=2] {'cells','rep'}, use_global_device_ids=true, to_apply=%region_34.0 | all-reduce | flops 1600 | bytes 12800 | tf_op jit(solution)/shard_map/psum | solution.py:60
  659.0 2.2 multiply_convert_fusion.2
  661.2 1.0 copy-done.20
  662.1 3.0 fusion.48
  665.1 5.9 concatenate.13
  671.0 5.2 pad_maximum_fusion
  676.2 1.5 copy-done.9
  677.8 18.7 %fusion.37 = f32[800,7000]{1,0:T(8,128)} fusion(f32[576,7000]{1,0:T(8,128)} %get-tuple-element.68, f32[576,800]{0,1:T(8,128)S(1)} %copy-done.9, f32[800]{0:T(1024)S(1)} %copy-done.37, f32[800]{0:T(1024)S(1)} %copy-done.34, f32[800]{0:T(1024)S(1)} %copy-done.29, f32[800]{0:T(1024)S(1)} %broadcast_multiply_fusion.8), kind=kOutput, calls=%fused_computation.120 | convolution fusion | flops 6463411200 | bytes 40384000 | tf_op jit(solution)/shard_map/dot_general | solution.py:19
  696.5 26.0 %reshape.199 = f32[6400,875]{1,0:T(8,128)} reshape(f32[800,7000]{1,0:T(8,128)} %fusion.37) | data formatting | bytes 44800000 | tf_op jit(solution)/shard_map/reshape | solution.py:185
  722.6 1.4 copy-done.3
  724.3 4.4 fusion.38
  728.7 42.8 %all-reduce.2 = (f32[800]{0:T(1024)S(1)}, f32[800]{0:T(1024)S(1)}, f32[200]{0:T(256)}, f32[7000]{0:T(1024)}) all-reduce(f32[800]{0:T(1024)S(1)} %get-tuple-element.12, f32[800]{0:T(1024)S(1)} %get-tuple-element.11, f32[200]{0:T(256)S(1)} %convert_reduce_fusion.1, ...), channel_id=1, replica_groups=mesh['cells'=16,'rep'=2] {'cells','rep'}, use_global_device_ids=true, to_apply=%region_38.0 | all-reduce | flops 8800 | bytes 70400 | tf_op jit(solution)/shard_map/psum | solution.py:60
  771.5 17.5 %convolution_bitcast_fusion = f32[7000,800]{0,1:T(8,128)} fusion(bf16[576,7000]{1,0:T(8,128)(2,1)} %param.15, f32[576,800]{0,1:T(8,128)} %get-tuple-element.66, f32[576,800]{0,1:T(8,128)S(1)} %copy-done.3, f32[800]{0:T(1024)S(1)} %broadcast_multiply_fusion, f32[800]{0:T(1024)S(1)} %broadcast_multiply_fusion.1, f32[800]{0:T(1024)S(1)} %get-tuple-element.46, ...), kind=kOutput, calls=%fused_computation.4 | convolution fusion | flops 6454425600 | bytes 34166400 | tf_op jit(solution)/shard_map/dot_general | solution.py:19
  789.0 25.5 %copy.51 = f32[7000,800]{1,0:T(8,128)} copy(f32[7000,800]{0,1:T(8,128)} %convolution_bitcast_fusion) | data formatting | bytes 44800000 | tf_op jit(solution)/shard_map/dot_general | solution.py:19
  814.5 32.9 %reshape.198 = f32[6400,875]{1,0:T(8,128)} reshape(f32[7000,800]{1,0:T(8,128)} %copy.51) | data formatting | bytes 44800000 | tf_op jit(solution)/shard_map/reshape | solution.py:186
  849.4 19.3 %multiply_subtract_fusion = f32[576,7000]{1,0:T(8,128)} fusion(f32[576,7000]{1,0:T(8,128)} %get-tuple-element.68, bf16[7000,800]{0,1:T(8,128)(2,1)} %param.20, f32[576,800]{0,1:T(8,128)} %get-tuple-element.66, f32[576,800]{0,1:T(8,128)S(1)} %copy-done.3, f32[800]{0:T(1024)S(1)} %broadcast_multiply_fusion, f32[800]{0:T(1024)S(1)} %broadcast_multiply_fusion.1, ...), kind=kOutput, calls=%fused_computation.1 | convolution fusion | flops 6466521600 | bytes 47158400 | tf_op jit(solution)/shard_map/dot_general | solution.py:25
  868.7 67.1 %reduce-scatter.10.cloned.1.call-done = f32[64,625]{1,0:T(8,128)} async-done(((f32[2048,625]{1,0:T(8,128)}), f32[64,625]{1,0:T(8,128)}) %reduce-scatter.10.cloned.1.call-update) | async-done | bytes 160016 | tf_op jit(solution)/shard_map/reduce_scatter | solution.py:193
  935.8 245.1 %reduce-scatter.14.cloned.1.call-done = f32[200,875]{1,0:T(8,128)} async-done(((f32[6400,875]{1,0:T(8,128)}), f32[200,875]{1,0:T(8,128)}) %reduce-scatter.14.cloned.1.call-update) | async-done | bytes 700016
  1181.0 254.3 %reduce-scatter.12.cloned.1.call-done = f32[200,875]{1,0:T(8,128)} async-done(((f32[6400,875]{1,0:T(8,128)}), f32[200,875]{1,0:T(8,128)}) %reduce-scatter.12.cloned.1.call-update) | async-done | bytes 700016
  1435.2 2.0 copy.56
  1437.2 1.8 copy.57
  (150 shorter events, 10.9 us)
Async XLA Ops:
  7.2 287.4 %copy-start = (bf16[800,800]{1,0:T(8,128)(2,1)S(1)}, bf16[800,800]{1,0:T(8,128)(2,1)}, u32[]{:S(2)}) copy-start(bf16[800,800]{1,0:T(8,128)(2,1)} %param.25) | copy-start | bytes 3840004
  11.3 282.3 %copy-start.26 = (f32[800]{0:T(1024)}, f32[800]{0:T(1024)S(1)}, u32[]{:S(2)}) copy-start(f32[800]{0:T(1024)S(1)} %get-tuple-element.26) | copy-start | bytes 9604
  24.7 83.6 %copy-start.2 = (f32[576,800]{0,1:T(8,128)}, f32[576,800]{0,1:T(8,128)S(1)}, u32[]{:S(2)}) copy-start(f32[576,800]{0,1:T(8,128)S(1)} %get-tuple-element.54) | copy-start | bytes 5529604
  107.3 1.4 copy-start.42
  108.6 2.8 copy-start.16
  111.4 82.7 %copy-start.4 = (f32[576,800]{0,1:T(8,128)S(1)}, f32[576,800]{0,1:T(8,128)}, u32[]{:S(2)}) copy-start(f32[576,800]{0,1:T(8,128)} %get-tuple-element.56) | copy-start | bytes 5529604
  153.5 42.7 %copy-start.41 = (f32[200]{0:T(256)S(1)}, f32[200]{0:T(256)}, u32[]{:S(2)}) copy-start(f32[200]{0:T(256)} %param.23) | copy-start | bytes 2404
  193.5 2.6 copy-start.23
  194.1 2.5 copy-start.24
  194.1 6.9 copy-start.38
  194.1 6.9 copy-start.44
  195.2 1.0 copy-start.6
  196.2 12.4 copy-start.14
  196.7 11.9 copy-start.10
  202.2 323.8 %all-to-all-start.1 = ((f32[16,4,2]{1,2,0:T(2,128)}), f32[16,4,2]{1,2,0:T(2,128)S(1)}, u32[]{:S(2)}, u32[]{:S(2)}) async-start(f32[16,4,2]{1,2,0:T(2,128)} %copy.48), calls=%async_computation.1 | async-start | bytes 32768 | tf_op jit(solution)/shard_map/all_to_all | solution.py:94
  208.7 0.7 copy-start.12
  294.6 2.8 copy-start.18
  382.8 19.8 %copy-start.33 = (f32[800]{0:T(1024)}, f32[800]{0:T(1024)S(1)}, u32[]{:S(2)}) copy-start(f32[800]{0:T(1024)S(1)} %get-tuple-element.52) | copy-start | bytes 9604
  382.8 19.8 %copy-start.8 = (f32[576,800]{0,1:T(8,128)S(1)}, f32[576,800]{0,1:T(8,128)}, u32[]{:S(2)}) copy-start(f32[576,800]{0,1:T(8,128)} %get-tuple-element.60) | copy-start | bytes 5529604
  382.8 19.8 %copy-start.28 = (f32[800]{0:T(1024)S(1)}, f32[800]{0:T(1024)}, u32[]{:S(2)}) copy-start(f32[800]{0:T(1024)} %get-tuple-element.19) | copy-start | bytes 9604
  382.8 19.8 %copy-start.36 = (f32[800]{0:T(1024)S(1)}, f32[800]{0:T(1024)}, u32[]{:S(2)}) copy-start(f32[800]{0:T(1024)} %get-tuple-element.23) | copy-start | bytes 9604
  464.0 2.8 copy-start.19
  466.8 3.0 copy-start.27
  514.3 2.4 copy-start.13
  514.3 3.6 copy-start.11
  514.3 3.6 copy-start.15
  514.3 3.6 copy-start.22
  516.6 2.3 copy-start.39
  516.7 2.3 copy-start.43
  516.7 2.3 copy-start.45
  519.9 95.1 %copy-start.40 = (s32[16,4]{0,1:T(4,128)S(1)}, s32[16,4]{0,1:T(4,128)}, u32[]{:S(2)}) copy-start(s32[16,4]{0,1:T(4,128)} %param.19) | copy-start | bytes 772
  519.9 95.1 %copy-start.46 = (s32[16,4]{0,1:T(4,128)S(1)}, s32[16,4]{0,1:T(4,128)}, u32[]{:S(2)}) copy-start(s32[16,4]{0,1:T(4,128)} %param.18) | copy-start | bytes 772
  519.9 96.8 %copy-start.7 = (bf16[576,800]{0,1:T(8,128)(2,1)S(1)}, bf16[576,800]{0,1:T(8,128)(2,1)}, u32[]{:S(2)}) copy-start(bf16[576,800]{0,1:T(8,128)(2,1)} %copy-done.6) | copy-start | bytes 2764804
  525.8 92.4 %copy-start.5 = (f32[576,800]{0,1:T(8,128)S(1)}, f32[576,800]{0,1:T(8,128)}, u32[]{:S(2)}) copy-start(f32[576,800]{0,1:T(8,128)} %get-tuple-element.56) | copy-start | bytes 5529604
  526.0 14.1 all-to-all-start
  532.6 336.1 %all-reduce.10.cloned.1.call-start = ((), (), s32[]{:S(2)}) async-start(), calls=%async_computation.8 | async-start | bytes 2179072 | tf_op jit(solution)/shard_map/psum | solution.py:182
  540.3 81.5 %copy-start.35 = (f32[4,1,100]{2,1,0:T(1,128)}, f32[4,1,100]{2,1,0:T(1,128)S(1)}, u32[]{:S(2)}) copy-start(f32[4,1,100]{2,1,0:T(1,128)S(1)} %get-tuple-element.44) | copy-start | bytes 4804
  618.2 40.7 %copy-start.32 = (f32[800]{0:T(1024)S(1)}, f32[800]{0:T(1024)}, u32[]{:S(2)}) copy-start(f32[800]{0:T(1024)} %get-tuple-element.47) | copy-start | bytes 9604
  658.9 277.0 %reduce-scatter.10.cloned.1.call-start = ((), (), s32[]{:S(2)}) async-start(), calls=%async_computation.5 | async-start | bytes 5406720 | tf_op jit(solution)/shard_map/reduce_scatter | solution.py:193
  658.9 3.2 copy-start.17
  661.1 1.0 copy-start.20
  676.2 1.6 copy-start.9
  676.2 1.6 copy-start.29
  676.2 1.6 copy-start.34
  676.2 1.6 copy-start.37
  676.2 504.8 %reduce-scatter.14.cloned.1.call-start = ((), (), s32[]{:S(2)}) async-start(), calls=%async_computation.7 | async-start | bytes 23654400
  722.4 1.6 copy-start.3
  722.4 1.8 copy-start.21
  722.5 712.8 %reduce-scatter.12.cloned.1.call-start = ((), (), s32[]{:S(2)}) async-start(), calls=%async_computation.6 | async-start | bytes 23654400
  724.3 4.5 copy-start.25
  847.4 0.7 copy-start.31
  847.4 0.7 copy-start.30
  849.4 589.5 %copy-start.1 = (bf16[800,800]{1,0:T(8,128)(2,1)S(1)}, bf16[800,800]{1,0:T(8,128)(2,1)}, u32[]{:S(2)}) copy-start(bf16[800,800]{1,0:T(8,128)(2,1)} %param.25) | copy-start | bytes 3840004
Sparse Core Ops, SparseCore 0:
  659.0 131.0 all-reduce.9
  793.0 142.7 reduce-scatter.9
  938.8 242.0 reduce-scatter.13
  1183.8 251.3 reduce-scatter.11
where the time goes:
time: 1460 us; the launch traced here: 1450 us
  waiting for transfers between devices  574 us (39%)
  blocking collectives  564 us (39%)
  matrix products  140 us (10%)
  local copies, waits for them, and re-layouts  112 us (8%)
  other arithmetic  28.5 us (2%)
  between operations  14.7 us (1%)
    unnamed x6, waiting for transfers between devices  499 us
    psum x4, blocking collectives, norm_forward(): column_sum = lax.psum(jnp.sum(values, axis=0), ('cells', 'rep'))  163 us
    psum x4, blocking collectives, norm_backward(): lax.psum((jnp.sum(grad_pre, axis=0), jnp.sum(grad_pre * normed, axis=0)),...  161 us
    psum x4, blocking collectives, norm_forward(): lax.psum(jnp.sum(centered * centered, axis=0), ('cells', 'rep'))  161 us
    reduce_scatter x1, waiting for transfers between devices, shards(): lax.psum_scatter(flat_narrow, ('cells', 'rep'), scatter_dimension=0, tile...  67.1 us
    dot_general x6, matrix products, contract_cols(): lax.dot_general(left, right, (((1,), (1,)), ((), ())), preferred_element_...  52.1 us
    dot_general x6, matrix products, contract_rows(): lax.dot_general(left, right, (((0,), (0,)), ((), ())), preferred_element_...  44.8 us
    psum x1, blocking collectives, group_terms(): offset_sum = lax.psum(jnp.sum(offset, axis=0), 'cells')  37.5 us
  transfers between devices with their start and end apart: 6, of which 4 were waited for; matrix products, arithmetic and copies ran while one was open for 16% of the time, Pallas kernels for 0%

commit v1 on v0

v1 whole, which is shorter than its diff:
```python
import functools

import jax
import jax.numpy as jnp
from jax import lax
from jax.experimental import pallas as pl
from jax.experimental.pallas import tpu as pltpu
from jax.sharding import PartitionSpec as P

POP_DEV = 2
FLAT_COLS = 875
NARROW_COLS = 625
FLAT_ROWS = 6400
NARROW_ROWS = 2048

NORM_EPSILON = 1e-05
KL_WEIGHT = 5e-05
OFFSET_WEIGHT = 200.0

MESH_ID = pl.DeviceIdType.MESH
WIN = 1024
ROWS = 48
F32 = jnp.float32
BF16 = jnp.bfloat16


class Slice:
    def __init__(self, cells, rep):
        self.cells, self.rep = cells, rep
        self.n = cells * rep
        self.bits = self.n.bit_length() - 1
        self.digits = []
        low = 0
        while low < self.bits:
            width = min(3, self.bits - low)
            self.digits.append((low, 1 << width))
            low += width

    def me(self):
        return lax.axis_index("cells") * self.rep + lax.axis_index("rep")

    def place(self, index):
        return (index // self.rep, index % self.rep)


def entry_barrier(grid, peers):
    barrier = pltpu.get_barrier_semaphore()
    for peer in peers:
        pl.semaphore_signal(barrier, inc=1, device_id=grid.place(peer), device_id_type=MESH_ID)
    pl.semaphore_wait(barrier, len(peers))


def digit_peers(grid):
    me = grid.me()
    peers = []
    for low, size in grid.digits:
        rank = (me // (1 << low)) % size
        for k in range(1, size):
            other = (rank + k) % size
            peers.append(me + (other - rank) * (1 << low))
    return peers


class Gather:
    def __init__(self, grid, buffers, send_sems, recv_sems):
        self.grid, self.buffers, self.send_sems, self.recv_sems = grid, buffers, send_sems, recv_sems

    def rank(self, level):
        low, size = self.grid.digits[level]
        return (self.grid.me() // (1 << low)) % size

    def copy(self, level, slot, k, arriving=False):
        low, size = self.grid.digits[level]
        rank = self.rank(level)
        to = (rank + k) % size
        buffer = self.buffers[level].at[slot]
        return pltpu.make_async_remote_copy(
            src_ref=buffer.at[rank],
            dst_ref=buffer.at[(rank + size - k) % size if arriving else rank],
            send_sem=self.send_sems[level].at[slot, k - 1],
            recv_sem=self.recv_sems[level].at[slot, k - 1],
            device_id=self.grid.place(self.grid.me() + (to - rank) * (1 << low)),
            device_id_type=MESH_ID,
        )

    def start(self, level, slot):
        for k in range(1, self.grid.digits[level][1]):
            self.copy(level, slot, k).start()

    def wait(self, level, slot):
        for k in range(1, self.grid.digits[level][1]):
            self.copy(level, slot, k, arriving=True).wait_recv()

    def finish(self, level, slot):
        for k in range(1, self.grid.digits[level][1]):
            self.copy(level, slot, k).wait_send()

    def own(self, level, slot):
        return self.buffers[level].at[slot, self.rank(level)]


def put_row(ref, first, row, width):
    full = width // 128
    for c in range(full):
        ref[first + c : first + c + 1, :] = row[:, 128 * c : 128 * (c + 1)]
    rest = width - 128 * full
    if rest:
        ref[first + full : first + full + 1, 0:rest] = row[:, 128 * full : width]


def take_row(block, first, width):
    pieces = []
    for c in range(-(-width // 128)):
        pieces.append(block[first + c : first + c + 1, 0 : min(128, width - 128 * c)])
    return jnp.concatenate(pieces, axis=1)


def row_loop(rows, body, init):
    steps = rows // ROWS

    def step(i, carry):
        return body(pl.ds(pl.multiple_of(i * ROWS, ROWS), ROWS), carry)

    return lax.fori_loop(0, steps, step, init)


def column_sum(value):
    return jnp.sum(value, axis=0, keepdims=True)


def batch_norm(pre, nrm_out, act_out, gather, slot, gain_row, shift_row, inv_out):
    rows, width = pre.shape
    total = row_loop(rows, lambda r, c: c + column_sum(pre[r, :]), jnp.zeros((1, width), F32))
    mean = total * (1.0 / rows)

    def squares(r, c):
        d = pre[r, :] - mean
        return c + column_sum(d * d)

    square = row_loop(rows, squares, jnp.zeros((1, width), F32))
    own = gather.own(0, slot)
    put_row(own, 0, mean, width)
    put_row(own, 8, square, width)
    count = float(rows)
    levels = len(gather.grid.digits)
    for level in range(levels):
        size = gather.grid.digits[level][1]
        gather.start(level, slot)
        gather.wait(level, slot)
        buffer = gather.buffers[level].at[slot]
        means = [buffer[g, 0:8, :] for g in range(size)]
        merged = sum(means[1:], means[0]) * (1.0 / size)
        spread = sum([buffer[g, 8:16, :] for g in range(1, size)], buffer[0, 8:16, :])
        between = sum([(m - merged) * (m - merged) for m in means[1:]], (means[0] - merged) * (means[0] - merged))
        spread = spread + count * between
        count = count * size
        if level + 1 < levels:
            own = gather.own(level + 1, slot)
            own[0:8, :] = merged
            own[8:16, :] = spread
    inv = lax.rsqrt(spread * (1.0 / count) + NORM_EPSILON)
    mean = take_row(merged, 0, width)
    inv = take_row(inv, 0, width)
    inv_out[...] = inv

    def write(r, c):
        nrm = (pre[r, :] - mean) * inv
        nrm_out[r, :] = nrm
        value = gain_row * nrm + shift_row
        act_out[r, :] = (value * jax.nn.sigmoid(value)).astype(BF16)
        return c

    row_loop(rows, write, 0)


def nt(left, right):
    return lax.dot_general(left, right, (((1,), (1,)), ((), ())), preferred_element_type=F32)


def nn(left, right):
    return lax.dot_general(left, right, (((1,), (0,)), ((), ())), preferred_element_type=F32)


def tn(left, right):
    return lax.dot_general(left, right, (((0,), (0,)), ((), ())), preferred_element_type=F32)


def exact(left, right, dims):
    return lax.dot_general(
        left, right, (dims, ((), ())), precision=lax.Precision.HIGHEST, preferred_element_type=F32
    )


def windows(width):
    return [(s, min(WIN, width - s)) for s in range(0, width, WIN)]


def part_of(full, tail, i):
    return full.at[i] if i < full.shape[0] else tail


def forward_kernel(
    grid,
    table_ref,
    mask_ref,
    x_hbm,
    w1_hbm,
    noise_ref,
    gid_ref,
    w2_ref,
    head_ref,
    headb_ref,
    d1_ref,
    d2_ref,
    gain_ref,
    shift_ref,
    nrm0,
    nrm1,
    nrm2,
    nrm3,
    inv_out,
    act1,
    act2,
    zlat,
    act3,
    act4,
    head_out,
    ggroup_out,
    offsets_out,
    x_win,
    x_tail,
    w_win,
    w_tail,
    pre,
    moments,
    *rest,
):
    levels = len(grid.digits)
    small = rest[:levels]
    wide = rest[levels : 2 * levels]
    s_send, s_recv, g_send, g_recv = (
        rest[2 * levels : 3 * levels],
        rest[3 * levels : 4 * levels],
        rest[4 * levels : 5 * levels],
        rest[5 * levels : 6 * levels],
    )
    in_sems = rest[6 * levels]
    gather = Gather(grid, small, s_send, s_recv)
    group_gather = Gather(grid, wide, g_send, g_recv)
    latent = d1_ref.shape[0]
    genes = x_hbm.shape[1]
    spans = windows(genes)

    loads = []
    for i, (s, size) in enumerate(spans):
        a = pltpu.make_async_copy(x_hbm.at[:, pl.ds(s, size)], part_of(x_win, x_tail, i), in_sems.at[0, i])
        b = pltpu.make_async_copy(w1_hbm.at[:, pl.ds(s, size)], part_of(w_win, w_tail, i), in_sems.at[1, i])
        a.start()
        b.start()
        loads.append((a, b))
    entry_barrier(grid, digit_peers(grid))

    for i, (s, size) in enumerate(spans):
        loads[i][0].wait()
        loads[i][1].wait()
        part = nt(part_of(x_win, x_tail, i)[...], part_of(w_win, w_tail, i)[...])
        pre[...] = part if i == 0 else pre[...] + part

    def norm(k, nrm, act):
        batch_norm(
            pre, nrm, act, gather, k, gain_ref[k : k + 1, :], shift_ref[k : k + 1, :], inv_out.at[k : k + 1, :]
        )

    norm(0, nrm0, act1)
    pre[...] = nn(act1[...], w2_ref[...])
    norm(1, nrm1, act2)
    head = nt(act2[...], head_ref[...]) + headb_ref[...]
    head_out[...] = head
    mu = head[:, 0:latent]
    logvar = head[:, latent : 2 * latent]
    zlat[...] = (mu + jnp.exp(0.5 * logvar) * noise_ref[...]).astype(BF16)

    groups = ggroup_out.shape[0]
    pops = groups // 2
    cells_here = gid_ref.shape[1]
    member = (lax.broadcasted_iota(jnp.int32, (groups, cells_here), 0) == gid_ref[...]).astype(F32)
    own = group_gather.own(0, 0)
    own[:, 0:latent] = exact(member, mu, ((1,), (0,)))
    own[:, latent : latent + 1] = jnp.sum(member, axis=1, keepdims=True)
    group_gather.start(0, 0)

    pre[...] = nn(zlat[...], d1_ref[...])
    norm(2, nrm2, act3)
    for level in range(levels):
        group_gather.wait(level, 0)
        size = grid.digits[level][1]
        buffer = wide[level].at[0]
        total = sum([buffer[g] for g in range(1, size)], buffer[0])
        if level + 1 < levels:
            group_gather.own(level + 1, 0)[...] = total
            group_gather.start(level + 1, 0)
        if level == 0:
            pre[...] = nn(act3[...], d2_ref[...])
            norm(3, nrm3, act4)
    counted = jnp.maximum(total[:, latent : latent + 1], 1.0)
    moments[...] = total / counted
    odd, even = pl.ds(1, pops, stride=2), pl.ds(0, pops, stride=2)
    offset = moments[odd, :] - moments[even, :]
    centre = jnp.sum(offset, axis=0, keepdims=True) * (1.0 / pops)
    grad_offset = (2.0 * OFFSET_WEIGHT / pops) * (offset - centre)
    row = lax.axis_index("cells")
    slots = offsets_out.shape[0]
    lane = lax.broadcasted_iota(jnp.int32, (1, pops), 1)
    picks = jnp.concatenate(
        [jnp.where(lane == table_ref[row, s], mask_ref[row, s].astype(F32), 0.0) for s in range(slots)], axis=0
    )
    offsets_out[...] = exact(picks, offset, ((1,), (0,)))[:, 0:latent]
    moments[odd, :] = grad_offset
    moments[even, :] = -grad_offset
    ggroup_out[...] = moments[...] / counted

    for level in range(levels):
        for k in range(4):
            gather.finish(level, k)
        group_gather.finish(level, 0)


def call_forward(grid, cells_x, w1t, noise, gid, table, mask, w2, headt, headb, d1, d2, gain, shift):
    rows, genes = cells_x.shape
    hidden = w2.shape[0]
    latent = d1.shape[0]
    groups = 2 * POP_DEV * grid.cells
    count = len(windows(genes))
    levels = len(grid.digits)
    vm = pl.BlockSpec(memory_space=pltpu.VMEM)
    hbm = pl.BlockSpec(memory_space=pl.ANY)
    sm = pl.BlockSpec(memory_space=pltpu.SMEM)
    wide_f = jax.ShapeDtypeStruct((rows, hidden), F32)
    wide_b = jax.ShapeDtypeStruct((rows, hidden), BF16)
    out_shape = (
        wide_f,
        wide_f,
        wide_f,
        wide_f,
        jax.ShapeDtypeStruct((4, hidden), F32),
        wide_b,
        wide_b,
        jax.ShapeDtypeStruct((rows, latent), BF16),
        wide_b,
        wide_b,
        jax.ShapeDtypeStruct((rows, 2 * latent), F32),
        jax.ShapeDtypeStruct((groups, 128), F32),
        jax.ShapeDtypeStruct((table.shape[1], latent), F32),
    )
    scratch = (
        [
            pltpu.VMEM((count - 1, rows, WIN), BF16),
            pltpu.VMEM((rows, genes - (count - 1) * WIN), BF16),
            pltpu.VMEM((count - 1, hidden, WIN), BF16),
            pltpu.VMEM((hidden, genes - (count - 1) * WIN), BF16),
            pltpu.VMEM((rows, hidden), F32),
            pltpu.VMEM((groups, 128), F32),
        ]
        + [pltpu.VMEM((4, size, 16, 128), F32) for _, size in grid.digits]
        + [pltpu.VMEM((1, size, groups, 128), F32) for _, size in grid.digits]
        + [pltpu.SemaphoreType.DMA((4, size - 1)) for _, size in grid.digits]
        + [pltpu.SemaphoreType.DMA((4, size - 1)) for _, size in grid.digits]
        + [pltpu.SemaphoreType.DMA((1, size - 1)) for _, size in grid.digits]
        + [pltpu.SemaphoreType.DMA((1, size - 1)) for _, size in grid.digits]
        + [pltpu.SemaphoreType.DMA((2, count))]
    )
    return pl.pallas_call(
        functools.partial(forward_kernel, grid),
        out_shape=out_shape,
        in_specs=[sm, sm, hbm, hbm] + [vm] * 9,
        out_specs=[vm] * len(out_shape),
        scratch_shapes=scratch,
        name="forward",
        compiler_params=pltpu.CompilerParams(
            collective_id=0, has_side_effects=True, vmem_limit_bytes=60 * 2**20
        ),
    )(table, mask, cells_x, w1t, noise, gid, w2, headt, headb, d1, d2, gain, shift)


def contract_rows(left, right):
    return lax.dot_general(left, right, (((0,), (0,)), ((), ())), preferred_element_type=F32)


def contract_cols(left, right):
    return lax.dot_general(left, right, (((1,), (1,)), ((), ())), preferred_element_type=F32)


def norm_backward(grad_act, normed, inv_std, norm_gain, norm_shift, cell_total):
    pre_act = norm_gain * normed + norm_shift
    gate_value = jax.nn.sigmoid(pre_act)
    grad_pre = grad_act * gate_value * (1.0 + pre_act * (1.0 - gate_value))
    grad_shift, grad_gain = lax.psum(
        (jnp.sum(grad_pre, axis=0), jnp.sum(grad_pre * normed, axis=0)), ("cells", "rep")
    )
    grad_in = norm_gain * inv_std * (grad_pre - grad_shift / cell_total - normed * (grad_gain / cell_total))
    return (grad_in.astype(BF16), grad_gain, grad_shift)


def shards(
    grid,
    cells_x,
    latent_noise,
    group_ids,
    owner_table,
    owner_mask,
    enc_w1,
    enc_w2,
    head_w,
    head_b,
    dec_w1,
    dec_w2,
    out_w,
    out_b,
    bn_gain,
    bn_shift,
):
    cell_total = float(cells_x.shape[0] * grid.n)
    latent_width = dec_w1.shape[0]
    gene_count = cells_x.shape[1]
    (nrm0, nrm1, nrm2, nrm3, inv, first_act, second_act, latent_draw, third_act, fourth_act, head_out, ggroup, offsets) = (
        call_forward(
            grid,
            cells_x,
            enc_w1.T,
            latent_noise,
            group_ids.reshape(1, -1),
            owner_table,
            owner_mask,
            enc_w2,
            head_w.T,
            head_b.reshape(1, -1),
            dec_w1,
            dec_w2,
            bn_gain,
            bn_shift,
        )
    )
    latent_mean = head_out[:, :latent_width]
    logvar = head_out[:, latent_width:]
    deviation = jnp.exp(0.5 * logvar)
    member = (group_ids[:, None] == jnp.arange(ggroup.shape[0], dtype=jnp.int32)[None, :]).astype(F32)
    grad_group = jnp.dot(member, ggroup, precision=lax.Precision.HIGHEST, preferred_element_type=F32)[:, :latent_width]
    residual = (
        jnp.dot(fourth_act, out_w, preferred_element_type=F32) + out_b - cells_x.astype(F32)
    )
    grad_recon = (residual * (2.0 / cell_total)).astype(BF16)
    grad_out_w = contract_rows(fourth_act, grad_recon)
    grad_out_b = jnp.sum(grad_recon.astype(F32), axis=0)
    grad_fourth = contract_cols(grad_recon, out_w)
    grad_pre4, gain_three, shift_three = norm_backward(grad_fourth, nrm3, inv[3], bn_gain[3], bn_shift[3], cell_total)
    grad_dec_w2 = contract_rows(third_act, grad_pre4)
    grad_third = contract_cols(grad_pre4, dec_w2)
    grad_pre3, gain_two, shift_two = norm_backward(grad_third, nrm2, inv[2], bn_gain[2], bn_shift[2], cell_total)
    grad_dec_w1 = contract_rows(latent_draw, grad_pre3)
    grad_latent = contract_cols(grad_pre3, dec_w1)
    kl_scale = KL_WEIGHT * gene_count / cell_total
    grad_mean = grad_latent + kl_scale * latent_mean + grad_group
    grad_logvar = grad_latent * latent_noise * (0.5 * deviation) + 0.5 * kl_scale * (jnp.exp(logvar) - 1.0)
    grad_head = jnp.concatenate([grad_mean, grad_logvar], axis=1).astype(BF16)
    grad_head_w = contract_rows(second_act, grad_head)
    grad_head_b = jnp.sum(grad_head.astype(F32), axis=0)
    grad_second = contract_cols(grad_head, head_w)
    grad_pre2, gain_one, shift_one = norm_backward(grad_second, nrm1, inv[1], bn_gain[1], bn_shift[1], cell_total)
    grad_enc_w2 = contract_rows(first_act, grad_pre2)
    grad_first = contract_cols(grad_pre2, enc_w2)
    grad_pre1, gain_zero, shift_zero = norm_backward(grad_first, nrm0, inv[0], bn_gain[0], bn_shift[0], cell_total)
    grad_enc_w1 = contract_rows(cells_x, grad_pre1)
    grad_x = cell_total * contract_cols(grad_pre1, enc_w1) - 2.0 * residual
    summed_head_b, summed_out_b, summed_head_w, summed_dec_w1 = lax.psum(
        (grad_head_b, grad_out_b, grad_head_w, grad_dec_w1), ("cells", "rep")
    )
    flat_out = grad_out_w.reshape(FLAT_ROWS, FLAT_COLS)
    flat_enc = grad_enc_w1.reshape(FLAT_ROWS, FLAT_COLS)
    flat_narrow = jnp.concatenate([grad_enc_w2.reshape(-1), grad_dec_w2.reshape(-1)]).reshape(
        NARROW_ROWS, NARROW_COLS
    )
    shard_out, shard_enc, shard_narrow = (
        lax.psum_scatter(flat_out, ("cells", "rep"), scatter_dimension=0, tiled=True),
        lax.psum_scatter(flat_enc, ("cells", "rep"), scatter_dimension=0, tiled=True),
        lax.psum_scatter(flat_narrow, ("cells", "rep"), scatter_dimension=0, tiled=True),
    )
    grad_gain = jnp.stack([gain_zero, gain_one, gain_two, gain_three])
    grad_shift = jnp.stack([shift_zero, shift_one, shift_two, shift_three])
    return (
        grad_x,
        shard_enc,
        shard_narrow,
        summed_head_w,
        summed_dec_w1,
        summed_head_b,
        shard_out,
        summed_out_b,
        grad_gain,
        grad_shift,
        offsets[None],
    )


def solution(mesh):
    grid = Slice(mesh.shape["cells"], mesh.shape["rep"])
    lines = P(("cells", "rep"), None)
    return jax.shard_map(
        functools.partial(shards, grid),
        mesh=mesh,
        in_specs=(lines, lines, P(("cells", "rep"))) + (P(),) * 12,
        out_specs=(lines, lines, lines, P(), P(), P(), lines, P(), P(), P(), P("cells", None, None)),
        check_vma=False,
    )
```

time: 1460 us -> 1000 us (0.68)
  blocking collectives: 564 us -> 161 us
  Pallas kernels: 0 us -> 61.6 us
  waiting for transfers between devices: 574 us -> 518 us
  matrix products: 140 us -> 110 us
    psum x10 -> x0, blocking collectives: 366 us -> none  [the longest x4 163 us: norm_forward(): column_sum = lax.psum(jnp.sum(values, axis=0), ('cells', 'rep'))]
    pallas_call x0 -> x1, Pallas kernels: none -> 61.6 us  [call_forward(): pl.pallas_call(functools.partial(forward_kernel, grid), out_shape=out_sha...]
    reduce_scatter x1, waiting for transfers between devices: 67.1 us -> 18.7 us  [shards(): lax.psum_scatter(flat_narrow, ('cells', 'rep'), scatter_dimension=0, tile...]
    all_gather x1 -> x0, blocking collectives: 36.8 us -> none  [group_terms(): lax.all_gather(grad_means.reshape(1, slot_count, 2 * latent_width), 'cell...]
    dot_general x11 -> x2, matrix products: 43.4 us -> 19.4 us  [the longest x1 18.1 us: shards(): jnp.dot(fourth_act, out_w, preferred_element_type=F32) + out_b]
  transfers between devices with their start and end apart: 6 -> 4, of which waited for: 4 -> 3; matrix products, arithmetic and copies ran while one was open for 16% -> 17% of each run, Pallas kernels for 0% -> 0%
where the time goes in v1:
time: 1000 us; the launch traced here: 993 us
  waiting for transfers between devices  518 us (52%)
  blocking collectives  161 us (16%)
  local copies, waits for them, and re-layouts  110 us (11%)
  matrix products  110 us (11%)
  Pallas kernels  61.6 us (6%)
  other arithmetic  16.5 us (2%)
  between operations  14.4 us (1%)
    unnamed x6, waiting for transfers between devices  499 us
    psum x4, blocking collectives, norm_backward(): lax.psum((jnp.sum(grad_pre, axis=0), jnp.sum(grad_pre * normed, axis=0)),...  161 us
    pallas_call x1, Pallas kernels, call_forward(): pl.pallas_call(functools.partial(forward_kernel, grid), out_shape=out_sha...  61.6 us
    dot_general x6, matrix products, contract_cols(): lax.dot_general(left, right, (((1,), (1,)), ((), ())), preferred_element_...  48.4 us
    dot_general x6, matrix products, contract_rows(): lax.dot_general(left, right, (((0,), (0,)), ((), ())), preferred_element_...  42.6 us
    reshape x1, local copies, waits for them, and re-layouts, shards(): flat_enc = grad_enc_w1.reshape(FLAT_ROWS, FLAT_COLS)  32.9 us
    reshape x1, local copies, waits for them, and re-layouts, shards(): flat_out = grad_out_w.reshape(FLAT_ROWS, FLAT_COLS)  26 us
    dot_general x1, local copies, waits for them, and re-layouts, contract_rows(): lax.dot_general(left, right, (((0,), (0,)), ((), ())), preferred_element_...  25.6 us
  transfers between devices with their start and end apart: 4, of which 3 were waited for; matrix products, arithmetic and copies ran while one was open for 17% of the time, Pallas kernels for 0%

profile of v1, /device:TPU:0, one launch (start us, length us, event | category | flops | bytes accessed | tf_op | source)
XLA Modules:
  0.0 992.6 jit_solution(1190325987648345720)
XLA Ops:
  7.2 0.0 all-reduce.9.cloned.1.call-start
  7.2 1.3 reshape.51.gid_ref
  8.5 1.4 copy.61.table_ref
  9.8 1.4 copy.62.mask_ref
  11.2 1.8 copy.63.noise_ref
  13.0 61.6 %forward.1 = (f32[576,800]{1,0:T(8,128)}, f32[576,800]{1,0:T(8,128)}, f32[576,800]{1,0:T(8,128)}, f32[576,800]{1,0:T(8,128)}, f32[4,800]{1,0:T(4,128)}, /*index=...) custom-call(s32[16,4]{1,0:T(8,128)} %copy.61.table_ref, ...), custom_call_target="tpu_custom_call" | custom-call | tf_op jit(solution)/shard_map/forward/pallas_call | solution.py:372
  74.6 0.0 copy-done.13
  74.7 1.0 slice_reduce_fusion
  75.7 18.1 %convert_reduce_fusion = (f32[7000]{0:T(1024)S(1)}, f32[576,7000]{1,0:T(8,128)}) fusion(bf16[576,7000]{1,0:T(8,128)(2,1)} %x_hbm.1, f32[7000]{0:T(1024)S(1)} %copy-done.19, bf16[576,800]{1,0:T(8,128)(2,1)} %get-tuple-element.25, bf16[800,7000]{1,0:T(8,128)(2,1)} %param.26), kind=kOutput, calls=%fused_computation | convolution fusion | flops 6479416832 | bytes 36369600 | tf_op jit(solution)/shard_map/dot_general | solution.py:449
  93.8 17.3 %fusion.10 = (f32[800]{0:T(1024)S(1)}, f32[800]{0:T(1024)S(1)}, f32[576,800]{1,0:T(8,128)}) fusion(f32[576,800]{1,0:T(8,128)S(1)} %copy-done.3, f32[800]{0:T(1024)S(1)} %get-tuple-element.55, f32[800]{0:T(1024)S(1)} %get-tuple-element.77, bf16[800,7000]{1,0:T(8,128)(2,1)} %param.26, f32[576,7000]{1,0:T(8,128)} %get-tuple-element.76), kind=kOutput, calls=%fused_computation.55 | convolution fusion | flops 6465252352 | bytes 31027200 | tf_op jit(solution)/shard_map/dot_general | solution.py:390
  111.1 39.1 %all-reduce.5 = (f32[800]{0:T(1024)S(1)}, f32[800]{0:T(1024)S(1)}) all-reduce(f32[800]{0:T(1024)S(1)} %get-tuple-element.44, f32[800]{0:T(1024)S(1)} %get-tuple-element.43), channel_id=1, replica_groups=mesh['cells'=16,'rep'=2] {'cells','rep'}, use_global_device_ids=true, to_apply=%region_3.0 | all-reduce | flops 1600 | bytes 12800 | tf_op jit(solution)/shard_map/psum | solution.py:397
  150.2 2.7 multiply_convert_fusion.4
  152.9 0.1 copy-done.2
  153.0 0.4 copy-done.4
  153.4 3.3 fusion.9
  156.7 40.1 %all-reduce.4 = (f32[800]{0:T(1024)S(1)}, f32[800]{0:T(1024)S(1)}) all-reduce(f32[800]{0:T(1024)S(1)} %get-tuple-element.42, f32[800]{0:T(1024)S(1)} %get-tuple-element.41), channel_id=1, replica_groups=mesh['cells'=16,'rep'=2] {'cells','rep'}, use_global_device_ids=true, to_apply=%region_7.0 | all-reduce | flops 1600 | bytes 12800 | tf_op jit(solution)/shard_map/psum | solution.py:397
  196.9 1.9 multiply_convert_fusion.3
  198.8 0.5 fusion.11
  199.4 0.0 copy-start.16
  199.4 0.4 copy-done.12
  199.7 1.1 fusion.14
  200.9 0.2 copy.68
  201.0 0.2 copy.66
  201.2 1.2 add_convert_fusion
  202.5 1.3 fusion
  203.8 1.6 fusion.2
  205.3 0.0 all-reduce.9.cloned.1.call-update
  205.4 0.2 reduce-scatter.10.cloned.1.call-start
  205.6 0.0 copy-start.11
  205.6 4.4 fusion.13
  210.0 2.5 fusion.8
  212.5 40.1 %all-reduce.3 = (f32[800]{0:T(1024)S(1)}, f32[800]{0:T(1024)S(1)}) all-reduce(f32[800]{0:T(1024)S(1)} %get-tuple-element.40, f32[800]{0:T(1024)S(1)} %get-tuple-element.39), channel_id=1, replica_groups=mesh['cells'=16,'rep'=2] {'cells','rep'}, use_global_device_ids=true, to_apply=%region_11.0 | all-reduce | flops 1600 | bytes 12800 | tf_op jit(solution)/shard_map/psum | solution.py:397
  252.6 2.0 multiply_convert_fusion.2
  254.6 1.0 copy-done.8
  255.6 3.1 fusion.12
  258.7 4.8 concatenate.14
  263.5 5.9 concatenate.13
  269.4 4.4 pad_maximum_fusion
  273.7 0.0 reduce-scatter.10.cloned.1.call-update
  273.8 0.0 reduce-scatter.14.cloned.1.call-start
  273.8 1.1 copy-done.6
  275.0 16.9 %fusion.6 = f32[800,7000]{1,0:T(8,128)} fusion(bf16[576,800]{1,0:T(8,128)(2,1)S(1)} %copy-done.6, f32[576,7000]{1,0:T(8,128)} %get-tuple-element.76), kind=kOutput, calls=%fused_computation.51 | convolution fusion | flops 6459264000 | bytes 39449600 | tf_op jit(solution)/shard_map/dot_general | solution.py:386
  291.8 26.0 %reshape.54 = f32[6400,875]{1,0:T(8,128)} reshape(f32[800,7000]{1,0:T(8,128)} %fusion.6) | data formatting | bytes 44800000 | tf_op jit(solution)/shard_map/reshape | solution.py:477
  317.8 0.0 reduce-scatter.14.cloned.1.call-update
  317.9 0.0 reduce-scatter.12.cloned.1.call-start
  317.9 0.2 convert_reduce_fusion.1
  318.1 1.3 copy-done
  319.4 0.3 copy-done.9
  319.7 4.6 fusion.7
  324.3 41.5 %all-reduce.2 = (f32[800]{0:T(1024)S(1)}, f32[800]{0:T(1024)S(1)}, f32[200]{0:T(256)}, f32[7000]{0:T(1024)}) all-reduce(f32[800]{0:T(1024)S(1)} %get-tuple-element.38, f32[800]{0:T(1024)S(1)} %get-tuple-element.37, f32[200]{0:T(256)S(1)} %convert_reduce_fusion.1, ...), channel_id=1, replica_groups=mesh['cells'=16,'rep'=2] {'cells','rep'}, use_global_device_ids=true, to_apply=%region_15.0 | all-reduce | flops 8800 | bytes 70400 | tf_op jit(solution)/shard_map/psum | solution.py:397
  365.8 1.9 multiply_convert_fusion.1
  367.7 15.6 %convolution_bitcast_fusion = f32[7000,800]{0,1:T(8,128)} fusion(bf16[576,800]{1,0:T(8,128)(2,1)S(1)} %multiply_convert_fusion.1, bf16[576,7000]{1,0:T(8,128)(2,1)} %x_hbm.1), kind=kOutput, calls=%fused_computation.4 | convolution fusion | flops 6451200000 | bytes 31385600 | tf_op jit(solution)/shard_map/dot_general | solution.py:386
  383.3 25.6 %copy.71 = f32[7000,800]{1,0:T(8,128)} copy(f32[7000,800]{0,1:T(8,128)} %convolution_bitcast_fusion) | data formatting | bytes 44800000 | tf_op jit(solution)/shard_map/dot_general | solution.py:386
  408.9 32.9 %reshape.53 = f32[6400,875]{1,0:T(8,128)} reshape(f32[7000,800]{1,0:T(8,128)} %copy.71) | data formatting | bytes 44800000 | tf_op jit(solution)/shard_map/reshape | solution.py:478
  441.8 0.0 reduce-scatter.12.cloned.1.call-update
  441.9 0.6 pad_maximum_fusion.4
  442.5 0.6 pad_maximum_fusion.5
  443.1 20.2 %multiply_subtract_fusion = f32[576,7000]{1,0:T(8,128)} fusion(f32[576,7000]{1,0:T(8,128)} %get-tuple-element.76, bf16[576,800]{1,0:T(8,128)(2,1)S(1)} %multiply_convert_fusion.1, bf16[7000,800]{0,1:T(8,128)(2,1)} %param.20), kind=kOutput, calls=%fused_computation.1 | convolution fusion | flops 6463296000 | bytes 44377600 | tf_op jit(solution)/shard_map/dot_general | solution.py:390
  463.3 18.7 %reduce-scatter.10.cloned.1.call-done = f32[64,625]{1,0:T(8,128)} async-done(((f32[2048,625]{1,0:T(8,128)}), f32[64,625]{1,0:T(8,128)}) %reduce-scatter.10.cloned.1.call-update) | async-done | bytes 160016 | tf_op jit(solution)/shard_map/reduce_scatter | solution.py:485
  482.0 245.0 %reduce-scatter.14.cloned.1.call-done = f32[200,875]{1,0:T(8,128)} async-done(((f32[6400,875]{1,0:T(8,128)}), f32[200,875]{1,0:T(8,128)}) %reduce-scatter.14.cloned.1.call-update) | async-done | bytes 700016
  727.1 254.3 %reduce-scatter.12.cloned.1.call-done = f32[200,875]{1,0:T(8,128)} async-done(((f32[6400,875]{1,0:T(8,128)}), f32[200,875]{1,0:T(8,128)}) %reduce-scatter.12.cloned.1.call-update) | async-done | bytes 700016
  981.3 2.0 copy.80
  983.3 1.8 copy.81
  985.1 0.6 copy.82
  (47 shorter events, 0.1 us)
Async XLA Ops:
  7.2 456.1 %all-reduce.9.cloned.1.call-start = ((), (), s32[]{:S(2)}) async-start(), calls=%async_computation.6 | async-start | bytes 2179072 | tf_op jit(solution)/shard_map/psum | solution.py:474
  13.0 61.6 %copy-start.13 = (f32[4,800]{1,0:T(4,128)S(1)}, f32[4,800]{1,0:T(4,128)}, u32[]{:S(2)}) copy-start(f32[4,800]{1,0:T(4,128)} %gain_ref.1) | copy-start | bytes 38404
  13.0 61.6 %copy-start.14 = (f32[4,800]{1,0:T(4,128)S(1)}, f32[4,800]{1,0:T(4,128)}, u32[]{:S(2)}) copy-start(f32[4,800]{1,0:T(4,128)} %shift_ref.1) | copy-start | bytes 38404
  13.0 62.6 %copy-start.19 = (f32[7000]{0:T(1024)S(1)}, f32[7000]{0:T(1024)}, u32[]{:S(2)}) copy-start(f32[7000]{0:T(1024)} %param.27) | copy-start | bytes 84004
  75.6 18.1 %copy-start.3 = (f32[576,800]{1,0:T(8,128)S(1)}, f32[576,800]{1,0:T(8,128)}, u32[]{:S(2)}) copy-start(f32[576,800]{1,0:T(8,128)} %get-tuple-element.26) | copy-start | bytes 5529604
  150.2 2.8 copy-start.2
  150.2 3.2 copy-start.4
  196.8 2.0 copy-start.5
  196.8 2.0 copy-start.10
  198.8 0.9 copy-start.12
  199.4 3.1 copy-start.15
  199.4 3.1 copy-start.16
  199.7 4.0 copy-start.7
  205.4 276.7 %reduce-scatter.10.cloned.1.call-start = ((), (), s32[]{:S(2)}) async-start(), calls=%async_computation.3 | async-start | bytes 5406720 | tf_op jit(solution)/shard_map/reduce_scatter | solution.py:485
  205.6 4.4 copy-start.1
  205.6 4.4 copy-start.11
  252.6 3.0 copy-start.18
  254.6 1.0 copy-start.8
  273.7 1.2 copy-start.6
  273.8 453.3 %reduce-scatter.14.cloned.1.call-start = ((), (), s32[]{:S(2)}) async-start(), calls=%async_computation.5 | async-start | bytes 23654400
  317.8 1.6 copy-start
  317.8 1.9 copy-start.9
  317.9 663.5 %reduce-scatter.12.cloned.1.call-start = ((), (), s32[]{:S(2)}) async-start(), calls=%async_computation.4 | async-start | bytes 23654400
  463.3 521.8 %copy-start.17 = (f32[4,100]{1,0:T(4,128)S(1)}, f32[4,100]{1,0:T(4,128)}, u32[]{:S(2)}) copy-start(f32[4,100]{1,0:T(4,128)} %get-tuple-element.36) | copy-start | bytes 4804
Sparse Core Ops, SparseCore 0:
  205.5 130.2 all-reduce.8
  338.8 143.2 reduce-scatter.9
  485.0 241.9 reduce-scatter.13
  729.9 251.3 reduce-scatter.11

commit v2 on v1

--- a/solution.py
+++ b/solution.py
@@ -382,23 +382,791 @@
     )(table, mask, cells_x, w1t, noise, gid, w2, headt, headb, d1, d2, gain, shift)
 
 
-def contract_rows(left, right):
-    return lax.dot_general(left, right, (((0,), (0,)), ((), ())), preferred_element_type=F32)
-
-
-def contract_cols(left, right):
-    return lax.dot_general(left, right, (((1,), (1,)), ((), ())), preferred_element_type=F32)
-
-
-def norm_backward(grad_act, normed, inv_std, norm_gain, norm_shift, cell_total):
-    pre_act = norm_gain * normed + norm_shift
-    gate_value = jax.nn.sigmoid(pre_act)
-    grad_pre = grad_act * gate_value * (1.0 + pre_act * (1.0 - gate_value))
-    grad_shift, grad_gain = lax.psum(
-        (jnp.sum(grad_pre, axis=0), jnp.sum(grad_pre * normed, axis=0)), ("cells", "rep")
-    )
-    grad_in = norm_gain * inv_std * (grad_pre - grad_shift / cell_total - normed * (grad_gain / cell_total))
-    return (grad_in.astype(BF16), grad_gain, grad_shift)
+ORDERS = ((0, 1, 2, 3, 4), (0, 2, 1, 3, 4), (0, 1, 3, 4, 2), (0, 2, 3, 4, 1))
+CHANNELS = len(ORDERS)
+PARTS = 32
+STAGES = 5
+SLOT_ROWS = 200
+
+
+class Scatter:
+    def __init__(self, grid, total, stage, low, landing, stage_sems, send_sems, recv_sems, credits):
+        self.grid, self.total = grid, total
+        self.stage, self.low, self.landing = stage, low, landing
+        self.stage_sems, self.send_sems, self.recv_sems, self.credits = stage_sems, send_sems, recv_sems, credits
+        self.shift = grid.bits - STAGES
+        self.rows = {}
+
+    def bit(self, b):
+        return (self.grid.me() // (1 << (b + self.shift))) % 2
+
+    def partner(self, b):
+        return self.grid.place(self.grid.me() + (1 - 2 * self.bit(b)) * (1 << (b + self.shift)))
+
+    def part(self, channel, k):
+        out = 0
+        for t, b in enumerate(ORDERS[channel]):
+            own = self.bit(b)
+            out = out + (1 << b) * ((1 - own) if (k >> (STAGES - 1 - t)) & 1 else own)
+        return out
+
+    def send(self, q, t):
+        channel, rows = q % CHANNELS, self.rows[q]
+        size = (16 >> t) * rows
+        if t == 0:
+            source, sem = self.stage.at[q % 2, 0:size], self.stage_sems.at[q % 2]
+        else:
+            source, sem = self.landing[t - 1].at[channel, size : 2 * size], self.send_sems.at[channel, t]
+        return pltpu.make_async_remote_copy(
+            src_ref=source,
+            dst_ref=self.landing[t].at[channel, 0:size],
+            send_sem=sem,
+            recv_sem=self.recv_sems.at[channel, t],
+            device_id=self.partner(ORDERS[channel][t]),
+            device_id_type=MESH_ID,
+        )
+
+    def start(self, q, t):
+        if q >= CHANNELS:
+            pl.semaphore_wait(self.credits.at[q % CHANNELS, t], 1)
+        self.send(q, t).start()
+
+    def free(self, q, t):
+        if q + CHANNELS < self.total:
+            channel = q % CHANNELS
+            pl.semaphore_signal(
+                self.credits.at[channel, t],
+                inc=1,
+                device_id=self.partner(ORDERS[channel][t]),
+                device_id_type=MESH_ID,
+            )
+
+    def upper(self, q, rows, fill):
+        self.rows[q] = rows
+        if q >= 2:
+            self.send(q - 2, 0).wait_send()
+        fill(self.stage.at[q % 2], True)
+        self.start(q, 0)
+
+    def lower(self, q, fill):
+        channel, rows = q % CHANNELS, self.rows[q]
+        fill(self.low, False)
+        self.send(q, 0).wait_recv()
+        mine = self.landing[0].at[channel]
+
+        def add(i, c):
+            r = pl.ds(pl.multiple_of(i * rows, 8), rows)
+            mine[r, :] += self.low[r, :]
+            return c
+
+        lax.fori_loop(0, 16, add, 0)
+        self.start(q, 1)
+
+    def fold(self, q, t):
+        channel, rows = q % CHANNELS, self.rows[q]
+        self.send(q, t).wait_recv()
+        mine, before = self.landing[t].at[channel], self.landing[t - 1].at[channel]
+
+        def add(i, c):
+            r = pl.ds(pl.multiple_of(i * rows, 8), rows)
+            mine[r, :] += before[r, :]
+            return c
+
+        lax.fori_loop(0, 16 >> t, add, 0)
+        self.send(q, t).wait_send()
+        self.free(q, t - 1)
+        self.start(q, t + 1)
+
+    def last(self, q, done):
+        channel, rows = q % CHANNELS, self.rows[q]
+        t = STAGES - 1
+        self.send(q, t).wait_recv()
+        done(self.landing[t][channel, 0:rows, :] + self.landing[t - 1][channel, 0:rows, :])
+        self.send(q, t).wait_send()
+        self.free(q, t - 1)
+        self.free(q, t)
+
+
+class Spread:
+    def __init__(self, scatter, block, landing, whole, sems):
+        self.scatter, self.block, self.landing, self.whole, self.sems = scatter, block, landing, whole, sems
+        self.rows = block.shape[0]
+
+    def begin(self, t):
+        out = 0
+        for i in range(t):
+            out = out + self.scatter.bit(i) * (self.rows >> (i + 1))
+        return out
+
+    def halving(self, t):
+        size = self.rows >> (t + 1)
+        at = self.begin(t) + (1 - self.scatter.bit(t)) * size
+        return pltpu.make_async_remote_copy(
+            src_ref=self.block.at[pl.ds(pl.multiple_of(at, 8), size)],
+            dst_ref=self.landing[t],
+            send_sem=self.sems.at[0, t],
+            recv_sem=self.sems.at[1, t],
+            device_id=self.scatter.partner(t),
+            device_id_type=MESH_ID,
+        )
+
+    def doubling(self, t, arriving=False):
+        size = self.rows >> (t + 1)
+        at = self.begin(t + 1)
+        there = self.begin(t) + (1 - self.scatter.bit(t)) * size if arriving else at
+        return pltpu.make_async_remote_copy(
+            src_ref=self.whole.at[pl.ds(pl.multiple_of(at, 8), size)],
+            dst_ref=self.whole.at[pl.ds(pl.multiple_of(there, 8), size)],
+            send_sem=self.sems.at[2, t],
+            recv_sem=self.sems.at[3, t],
+            device_id=self.scatter.partner(t),
+            device_id_type=MESH_ID,
+        )
+
+    def step(self, i):
+        if i == 0:
+            self.halving(0).start()
+        elif i <= STAGES:
+            t = i - 1
+            self.halving(t).wait_recv()
+            size = self.rows >> (t + 1)
+            r = pl.ds(pl.multiple_of(self.begin(t + 1), 8), size)
+            target = self.whole if i == STAGES else self.block
+            target[r, :] = self.block[r, :] + self.landing[t][...]
+            self.halving(t).wait_send()
+            if i < STAGES:
+                self.halving(t + 1).start()
+            else:
+                self.doubling(t).start()
+        else:
+            t = 2 * STAGES - i
+            self.doubling(t, True).wait_recv()
+            self.doubling(t).wait_send()
+            if t > 0:
+                self.doubling(t - 1).start()
+
+
+def one_hot(rows, target):
+    lane = lax.broadcasted_iota(jnp.int32, (rows, target.shape[1]), 0)
+    return jnp.where(lane == target, 1.0, 0.0).astype(BF16)
+
+
+def column_parts(width, size):
+    column = lax.broadcasted_iota(jnp.int32, (1, width), 1)
+    part = jnp.zeros((1, width), jnp.int32)
+    for m in range(1, width // size):
+        part = part + jnp.where(column >= m * size, 1, 0)
+    return column, part
+
+
+def slot_of(scatter, channel, bits, parts, part):
+    order = [b for b in ORDERS[channel] if b in bits]
+    slot = jnp.zeros_like(part)
+    for value in range(parts):
+        at = 0
+        for t, b in enumerate(order):
+            own = scatter.bit(b)
+            weight = 1 << (len(order) - 1 - t)
+            at = at + weight * ((1 - own) if (value >> bits.index(b)) & 1 else own)
+        slot = jnp.where(part == value, at, slot)
+    return slot
+
+
+def sum_blocks(gather, slot, idle):
+    levels = len(gather.grid.digits)
+    for level in range(levels):
+        gather.start(level, slot)
+        if level < len(idle):
+            idle[level]()
+        gather.wait(level, slot)
+        size = gather.grid.digits[level][1]
+        buffer = gather.buffers[level].at[slot]
+        total = sum([buffer[g] for g in range(1, size)], buffer[0])
+        if level + 1 < levels:
+            gather.own(level + 1, slot)[...] = total
+    return total
+
+
+def norm_gradient(grad, nrm, out, gather, slot, gain_row, shift_row, inv_row, scale, gain_out, shift_out, idle):
+    rows, width = grad.shape
+
+    def gate(r, carry):
+        n = nrm[r, :]
+        value = gain_row * n + shift_row
+        sig = jax.nn.sigmoid(value)
+        g = grad[r, :] * sig * (1.0 + value * (1.0 - sig))
+        grad[r, :] = g
+        return carry[0] + column_sum(g), carry[1] + column_sum(g * n)
+
+    zero = jnp.zeros((1, width), F32)
+    shift_sum, gain_sum = row_loop(rows, gate, (zero, zero))
+    own = gather.own(0, slot)
+    put_row(own, 0, shift_sum, width)
+    put_row(own, 8, gain_sum, width)
+    total = sum_blocks(gather, slot, idle)
+    shift_sum = take_row(total, 0, width)
+    gain_sum = take_row(total, 8, width)
+    shift_out[...] = shift_sum
+    gain_out[...] = gain_sum
+    factor = gain_row * inv_row
+    shift_mean = shift_sum * scale
+    gain_mean = gain_sum * scale
+
+    def write(r, c):
+        out[r, :] = (factor * (grad[r, :] - shift_mean - nrm[r, :] * gain_mean)).astype(BF16)
+        return c
+
+    row_loop(rows, write, 0)
+
+
+D1_ROWS = 104
+REP_ROWS = 2304
+
+
+def backward_kernel(
+    grid,
+    latent,
+    x_hbm,
+    outw_hbm,
+    nrm_hbm0,
+    nrm_hbm1,
+    nrm_hbm2,
+    nrm_hbm3,
+    act1_hbm,
+    act2_hbm,
+    act3_hbm,
+    act4_ref,
+    zlat_ref,
+    head_ref_in,
+    noise_ref,
+    gid_ref,
+    ggroup_ref,
+    inv_ref,
+    outb_ref,
+    w2_ref,
+    head_ref,
+    d1_ref,
+    d2_ref,
+    gain_ref,
+    shift_ref,
+    g_out,
+    gpre1,
+    out25,
+    enc_part,
+    nar_part,
+    d1_out,
+    headw_out,
+    outb_out,
+    headb_out,
+    gain_out,
+    shift_out,
+    *rest,
+):
+    levels = len(grid.digits)
+    rest = list(rest)
+
+    def take(n):
+        got = rest[:n]
+        del rest[:n]
+        return got
+
+    small, s_send, s_recv = take(levels), take(levels), take(levels)
+    stage, low, *landing = take(2 + STAGES)
+    stage_sems, send_sems, recv_sems, credits = take(4)
+    rep_block, rep_whole, *rep_landing = take(2 + STAGES)
+    (rep_sems,) = take(1)
+    g_win, wide, gact, gpre4, gpre3, gpre2, ghead, gcell, lhs, nrm_buf, fin = take(11)
+    picked = lhs.at[0:512]
+    in_sems, g_sems, nrm_sems, x_sems, act_sems = take(5)
+
+    rows, genes = x_hbm.shape
+    hidden = w2_ref.shape[0]
+    spans = windows(genes)
+    count = len(spans)
+    cell_total = float(rows * grid.n)
+    total = 2 * count + 2
+    gather = Gather(grid, small, s_send, s_recv)
+    scatter = Scatter(grid, total, stage, low, landing, stage_sems, send_sems, recv_sems, credits)
+    spread = Spread(scatter, rep_block, rep_landing, rep_whole, rep_sems)
+    rep_outb = 7 * (D1_ROWS + 2 * latent)
+    rep_headb = rep_outb + 8 * count
+
+    entry_barrier(grid, digit_peers(grid))
+    nrm_loads = {
+        k: pltpu.make_async_copy(ref, nrm_buf.at[(k + 1) % 2], nrm_sems.at[k])
+        for k, ref in enumerate((nrm_hbm0, nrm_hbm1, nrm_hbm2, nrm_hbm3))
+    }
+    nrm_loads[3].start()
+    nrm_loads[2].start()
+
+
+    def out_fill(s):
+        buffer = g_win.at[s % 3]
+
+        def fill(target, is_upper):
+            first = hidden // 2 if is_upper else 0
+            part = nn(lhs[first : first + hidden // 2, :], buffer[...])
+            for c in range(WIN // 128):
+                target[pl.ds(c, hidden // 2, stride=8), :] = part[:, 128 * c : 128 * (c + 1)]
+
+        return fill
+
+    def out_lhs(q):
+        column, part = column_parts(hidden, hidden // PARTS)
+        slot = slot_of(scatter, q % CHANNELS, (0, 1, 2, 3, 4), PARTS, part)
+        target = column + (hidden // PARTS) * (slot - part)
+        block = hidden // 5
+
+        def some(i, c):
+            at = pl.multiple_of(i * block, block)
+            lhs[pl.ds(at, block), :] = nt(one_hot(block, target - at), act4_ref[...]).astype(BF16)
+            return c
+
+        lax.fori_loop(0, 5, some, 0)
+
+    def out_piece(s):
+        out_lhs(s)
+        made(s, SLOT_ROWS, out_fill(s))
+
+    done = {}
+    state = {}
+
+    def reach(q, t):
+        while q in state and state[q] <= t:
+            stage_now = state[q]
+            if stage_now < STAGES - 1:
+                reach(q - CHANNELS, min(stage_now + 2, STAGES - 1))
+                scatter.fold(q, stage_now)
+            else:
+                scatter.last(q, done[q])
+            state[q] = stage_now + 1
+
+    def fold(q, t):
+        reach(q, t)
+
+    def made(q, rows_here, fill):
+        reach(q - CHANNELS, 1)
+        scatter.upper(q, rows_here, fill)
+        reach(q - CHANNELS, 2)
+        scatter.lower(q, fill)
+        state[q] = 1
+
+    def out_done(s):
+        def done(value):
+            fin[...] = value
+            for c in range(WIN // 128):
+                out25[:, WIN * s + 128 * c : WIN * s + 128 * (c + 1)] = fin[pl.ds(c, hidden // PARTS, stride=8), :]
+
+        return done
+
+    for s in range(count):
+        done[s] = out_done(s)
+
+    def output_layer(w_ring, w_tail, x_ring, x_tail):
+        def load(s):
+            at, size = spans[s]
+            tail = s == count - 1
+            return (
+                pltpu.make_async_copy(
+                    outw_hbm.at[:, pl.ds(at, size)], w_tail if tail else w_ring.at[s % 3], in_sems.at[0, s]
+                ),
+                pltpu.make_async_copy(
+                    x_hbm.at[:, pl.ds(at, size)], x_tail if tail else x_ring.at[s % 2], in_sems.at[1, s]
+                ),
+            )
+
+        def save(s):
+            return pltpu.make_async_copy(g_win.at[s % 3], g_out.at[:, pl.ds(WIN * s, WIN)], g_sems.at[s])
+
+        for s in range(2):
+            for copy in load(s):
+                copy.start()
+        for s, (at, size) in enumerate(spans):
+            tail = s == count - 1
+            w = w_tail if tail else w_ring.at[s % 3]
+            x = x_tail if tail else x_ring.at[s % 2]
+            for copy in load(s):
+                copy.wait()
+            wide[:, 0:size] = nn(act4_ref[...], w[...])
+            bias = outb_ref[:, at : at + size]
+            if s >= 3:
+                save(s - 3).wait()
+            g = g_win.at[s % 3]
+
+            def residual(r, c):
+                value = wide[r, 0:size] + bias - x[r, :].astype(F32)
+                value = (value * (2.0 / cell_total)).astype(BF16)
+                g[r, 0:size] = value
+                return c + column_sum(value.astype(F32))
+
+            put_row(rep_block, rep_outb + 8 * s, row_loop(rows, residual, jnp.zeros((1, size), F32)), size)
+            if size < WIN:
+                g[:, size:WIN] = jnp.zeros((rows, WIN - size), BF16)
+            save(s).start()
+            if s + 2 < count:
+                for copy in load(s + 2):
+                    copy.start()
+            if s < CHANNELS:
+                out_piece(s)
+            part = nt(g[:, 0:size], w[...])
+            gact[...] = part if s == 0 else gact[...] + part
+            if s == count - 2:
+                fold(0, 1)
+        for s in range(count - 3, count):
+            save(s).wait()
+
+    pl.run_scoped(
+        output_layer,
+        pltpu.VMEM((3, hidden, WIN), BF16),
+        pltpu.VMEM((hidden, spans[-1][1]), BF16),
+        pltpu.VMEM((2, rows, WIN), BF16),
+        pltpu.VMEM((rows, spans[-1][1]), BF16),
+    )
+
+
+    def pack(target, at, source, row, height):
+        full = hidden // 128
+        for c in range(full):
+            target[pl.ds(pl.multiple_of(at + height * c, 8), height), :] = source[
+                pl.ds(row, height), 128 * c : 128 * (c + 1)
+            ]
+        rest_width = hidden - 128 * full
+        pieces = [source[pl.ds(row + 8 * i, 8), 128 * full : hidden] for i in range(height // 8)]
+        target[pl.ds(pl.multiple_of(at + height * full, 8), 8), 0 : rest_width * len(pieces)] = jnp.concatenate(
+            pieces, axis=1
+        )
+
+    def unpack(value, out, row, height):
+        full = hidden // 128
+        rest_width = hidden - 128 * full
+        for c in range(full):
+            out[row : row + height, 128 * c : 128 * (c + 1)] = value[height * c : height * (c + 1), :]
+        for i in range(height // 8):
+            out[row + 8 * i : row + 8 * i + 8, 128 * full : hidden] = value[
+                height * full : height * full + 8, rest_width * i : rest_width * (i + 1)
+            ]
+
+    def finish(xt, x_part, x_last, act_buf):
+        window = x_part.shape[2]
+        height = xt.shape[1]
+        starts = [(genes * j) // PARTS for j in range(PARTS)]
+
+        def x_place(j):
+            at = starts[j] // 128 * 128
+            return (at, window) if at + window <= genes else (at, genes - at)
+
+        def x_load(j):
+            at, size = x_place(j)
+            target = x_part.at[j % 3] if size == window else x_last
+            return pltpu.make_async_copy(x_hbm.at[:, pl.ds(at, size)], target, x_sems.at[j])
+
+        def transpose(j):
+            x_load(j).wait()
+            at, size = x_place(j)
+            source = x_part.at[j % 3] if size == window else x_last
+            lane = lax.broadcasted_iota(jnp.int32, (height, size), 1)
+            line = lax.broadcasted_iota(jnp.int32, (height, size), 0)
+            select = jnp.where(lane == line + (starts[j] - at), 1.0, 0.0).astype(BF16)
+            xt[j] = nt(select, source[...]).astype(BF16)
+            if j + 3 < PARTS:
+                x_load(j + 3).start()
+
+        def transposes(first, number):
+            def run():
+                for j in range(first, first + number):
+                    transpose(j)
+
+            return run
+
+        def enc_fill(q, s):
+            def fill(target, is_upper):
+                for i in range(16):
+                    j = scatter.part(q % CHANNELS, 16 + i if is_upper else i)
+                    picked[32 * i : 32 * i + 32, :] = xt[j, 32 * s : 32 * s + 32, :]
+                wide[0:512, 0:hidden] = nn(picked[...], gpre1[...])
+
+                def one(i, c):
+                    pack(target, i * SLOT_ROWS, wide, pl.multiple_of(i * 32, 32), 32)
+                    return c
+
+                lax.fori_loop(0, 16, one, 0)
+
+            return fill
+
+        def enc_piece(q, s):
+            made(q, SLOT_ROWS, enc_fill(q, s))
+
+        def enc_done(s):
+            return lambda value: unpack(value, enc_part, 32 * s, 32)
+
+        each = 2 * hidden // PARTS
+        skip = (0, 32)
+
+        def nar_fill(q, which):
+            height_here = 32 if which == 0 else 24
+            rows_here = 25 * 8 if which == 0 else 19 * 8
+            channel = q % CHANNELS
+            place = STAGES - 1 - ORDERS[channel].index(4)
+
+            def fill(target, is_upper):
+                column, part = column_parts(hidden, each)
+                slot = slot_of(scatter, channel, (0, 1, 2, 3), PARTS // 2, part)
+                line = column - each * part - skip[which]
+                inside = (line >= 0) & (line < height_here)
+                base = 8 if is_upper else 0
+                place_in = jnp.where(inside, (slot - base) * height_here + line, -1)
+                place_in = jnp.where((slot >= base) & (slot < base + 8), place_in, -1)
+                select = one_hot(8 * height_here, place_in)
+                for matrix, act_slot, grad in ((0, 0, gpre2), (1, 1, gpre4)):
+                    size = 8 * height_here
+                    picked[0:size, :] = nt(select, act_buf[act_slot]).astype(BF16)
+                    wide[0:size, 0:hidden] = nn(picked[0:size, :], grad[...])
+                    flip = scatter.bit(4) if matrix == 0 else 1 - scatter.bit(4)
+                    for i in range(8):
+                        k = (i >> place) * (2 << place) + (i & ((1 << place) - 1)) + flip * (1 << place)
+                        pack(target, k * rows_here, wide, i * height_here, height_here)
+
+            return rows_here, fill
+
+        def nar_piece(q, which):
+            rows_here, fill = nar_fill(q, which)
+            made(q, rows_here, fill)
+
+        def nar_done(which):
+            if which == 0:
+                return lambda value: unpack(value, nar_part, 0, 32)
+            return lambda value: unpack(value, nar_part, 32, 24)
+
+        first = count
+        done[first] = nar_done(0)
+        done[first + 1] = nar_done(1)
+        for s in range(count):
+            done[first + 2 + s] = enc_done(s)
+
+        def row(ref, k):
+            return ref[k : k + 1, :]
+
+        def back(k, grad, out, idle):
+            nrm_loads[k].wait()
+            norm_gradient(
+                grad,
+                nrm_buf.at[(k + 1) % 2],
+                out,
+                gather,
+                k,
+                row(gain_ref, k),
+                row(shift_ref, k),
+                row(inv_ref, k),
+                1.0 / cell_total,
+                gain_out.at[k : k + 1, :],
+                shift_out.at[k : k + 1, :],
+                idle,
+            )
+
+        act_loads = [
+            pltpu.make_async_copy(ref, act_buf.at[at], act_sems.at[i])
+            for i, (ref, at) in enumerate(((act1_hbm, 0), (act3_hbm, 1), (act2_hbm, 0)))
+        ]
+        act_loads[1].start()
+        act_loads[2].start()
+        for j in range(3):
+            x_load(j).start()
+
+        groups = ggroup_ref.shape[0]
+        member = (lax.broadcasted_iota(jnp.int32, (groups, rows), 0) == gid_ref[...]).astype(F32)
+        gcell[...] = exact(member, ggroup_ref[...], ((0,), (0,)))
+
+        back(3, gact, gpre4, [transposes(0, 4), transposes(4, 4)])
+        nrm_loads[1].start()
+        gact[...] = nt(gpre4[...], d2_ref[...])
+        fold(1, 1)
+        back(2, gact, gpre3, [transposes(8, 4), transposes(12, 4)])
+        nrm_loads[0].start()
+        grad_z = nt(gpre3[...], d1_ref[...])
+        mu = head_ref_in[:, 0:latent]
+        logvar = head_ref_in[:, latent : 2 * latent]
+        kl = KL_WEIGHT * genes / cell_total
+        deviation = jnp.exp(0.5 * logvar)
+        grad_mu = grad_z + kl * mu + gcell[:, 0:latent]
+        grad_logvar = grad_z * noise_ref[...] * (0.5 * deviation) + 0.5 * kl * (jnp.exp(logvar) - 1.0)
+        ghead[...] = jnp.concatenate([grad_mu, grad_logvar], axis=1).astype(BF16)
+        gact[...] = nn(ghead[...], head_ref[...])
+        fold(0, 2)
+        out_piece(4)
+        fold(2, 1)
+
+        def latent_side():
+            act_loads[2].wait()
+            d1_grad = tn(zlat_ref[...], gpre3[...])
+            headw_grad = tn(ghead[...], act_buf[0])
+            act_loads[0].start()
+            for c in range(-(-hidden // 128)):
+                size = min(128, hidden - 128 * c)
+                at = D1_ROWS * c
+                rep_block[at : at + latent, 0:size] = d1_grad[:, 128 * c : 128 * c + size]
+                at = 7 * D1_ROWS + 2 * latent * c
+                rep_block[at : at + 2 * latent, 0:size] = headw_grad[:, 128 * c : 128 * c + size]
+            put_row(rep_block, rep_headb, column_sum(ghead[...].astype(F32)), 2 * latent)
+            spread.step(0)
+
+        back(1, gact, gpre2, [transposes(16, 4), transposes(20, 4)])
+        gact[...] = nt(gpre2[...], w2_ref[...])
+        latent_side()
+        fold(1, 2)
+        out_piece(5)
+        fold(3, 1)
+        back(0, gact, gpre1, [transposes(24, 4), transposes(28, 4)])
+        fold(0, 3)
+        fold(2, 2)
+        out_piece(6)
+        for copy in act_loads[:2]:
+            copy.wait()
+
+        steps = list(range(1, 2 * STAGES + 1))
+        for q in range(count, total):
+            if q < first + 2:
+                nar_piece(q, q - first)
+            else:
+                enc_piece(q, q - first - 2)
+            for lag, t in ((3, 1), (4, 2), (5, 3), (6, 4)):
+                if q - lag >= 0:
+                    fold(q - lag, t)
+            if steps:
+                spread.step(steps.pop(0))
+        for q in range(total, total + 6):
+            for lag, t in ((6, 4), (5, 3), (4, 2), (3, 1)):
+                if 0 <= q - lag < total:
+                    fold(q - lag, t)
+            if steps:
+                spread.step(steps.pop(0))
+        for i in steps:
+            spread.step(i)
+        for q in (total - 2, total - 1):
+            scatter.send(q, 0).wait_send()
+        for c in range(-(-hidden // 128)):
+            size = min(128, hidden - 128 * c)
+            at = D1_ROWS * c
+            d1_out[:, 128 * c : 128 * c + size] = rep_whole[at : at + latent, 0:size]
+            at = 7 * D1_ROWS + 2 * latent * c
+            headw_out[:, 128 * c : 128 * c + size] = rep_whole[at : at + 2 * latent, 0:size]
+        outb_out[...] = rep_whole[rep_outb : rep_outb + 8 * count, :]
+        headb_out[...] = rep_whole[rep_headb : rep_headb + 8, :]
+        for level in range(levels):
+            for k in range(4):
+                gather.finish(level, k)
+
+    last = genes - (genes * (PARTS - 1)) // PARTS // 128 * 128
+    pl.run_scoped(
+        finish,
+        pltpu.VMEM((PARTS, 224, rows), BF16),
+        pltpu.VMEM((3, rows, 384), BF16),
+        pltpu.VMEM((rows, last), BF16),
+        pltpu.VMEM((2, rows, hidden), BF16),
+    )
+
+
+def call_backward(grid, kept, cells_x, out_w, noise, gid, out_b, w2, headt, d1, d2, gain, shift):
+    (nrm0, nrm1, nrm2, nrm3, inv, act1, act2, zlat, act3, act4, head, ggroup) = kept
+    rows, genes = cells_x.shape
+    hidden, latent = w2.shape[0], d1.shape[0]
+    spans = windows(genes)
+    count = len(spans)
+    vm = pl.BlockSpec(memory_space=pltpu.VMEM)
+    hbm = pl.BlockSpec(memory_space=pl.ANY)
+    shape = jax.ShapeDtypeStruct
+    out_shape = (
+        shape((rows, WIN * count), BF16),
+        shape((rows, hidden), BF16),
+        shape((hidden // PARTS, WIN * count), F32),
+        shape((32 * count, hidden), F32),
+        shape((56, hidden), F32),
+        shape((latent, hidden), F32),
+        shape((2 * latent, hidden), F32),
+        shape((8 * count, 128), F32),
+        shape((8, 128), F32),
+        shape((4, hidden), F32),
+        shape((4, hidden), F32),
+    )
+    dma = pltpu.SemaphoreType.DMA
+    scratch = (
+        [pltpu.VMEM((4, size, 16, 128), F32) for _, size in grid.digits]
+        + [dma((4, size - 1)) for _, size in grid.digits]
+        + [dma((4, size - 1)) for _, size in grid.digits]
+        + [pltpu.VMEM((2, 16 * SLOT_ROWS, 128), F32), pltpu.VMEM((16 * SLOT_ROWS, 128), F32)]
+        + [pltpu.VMEM((CHANNELS, (16 >> t) * SLOT_ROWS, 128), F32) for t in range(STAGES)]
+        + [dma((2,)), dma((CHANNELS, STAGES)), dma((CHANNELS, STAGES)), pltpu.SemaphoreType.REGULAR((CHANNELS, STAGES))]
+        + [pltpu.VMEM((REP_ROWS, 128), F32), pltpu.VMEM((REP_ROWS, 128), F32)]
+        + [pltpu.VMEM((REP_ROWS >> (t + 1), 128), F32) for t in range(STAGES)]
+        + [dma((4, STAGES))]
+        + [
+            pltpu.VMEM((3, rows, WIN), BF16),
+            pltpu.VMEM((rows, WIN), F32),
+            pltpu.VMEM((rows, hidden), F32),
+            pltpu.VMEM((rows, hidden), BF16),
+            pltpu.VMEM((rows, hidden), BF16),
+            pltpu.VMEM((rows, hidden), BF16),
+            pltpu.VMEM((rows, 2 * latent), BF16),
+            pltpu.VMEM((rows, 128), F32),
+            pltpu.VMEM((hidden, rows), BF16),
+            pltpu.VMEM((2, rows, hidden), F32),
+            pltpu.VMEM((SLOT_ROWS, 128), F32),
+        ]
+        + [dma((2, count)), dma((count,)), dma((4,)), dma((PARTS,)), dma((3,))]
+    )
+    return pl.pallas_call(
+        functools.partial(backward_kernel, grid, latent),
+        out_shape=out_shape,
+        in_specs=[hbm] * 9 + [vm] * 14,
+        out_specs=[hbm] + [vm] * (len(out_shape) - 1),
+        scratch_shapes=scratch,
+        name="backward",
+        compiler_params=pltpu.CompilerParams(
+            collective_id=1, has_side_effects=True, vmem_limit_bytes=62 * 2**20
+        ),
+    )(
+        cells_x,
+        out_w,
+        nrm0,
+        nrm1,
+        nrm2,
+        nrm3,
+        act1,
+        act2,
+        act3,
+        act4,
+        zlat,
+        head,
+        noise,
+        gid,
+        ggroup,
+        inv,
+        out_b,
+        w2,
+        headt,
+        d1,
+        d2,
+        gain,
+        shift,
+    )
+
+
+def flat_shard(grid, flat, columns, rows_in_all):
+    value = flat.reshape(rows_in_all // PARTS, columns)
+    size = grid.n // PARTS
+    if size > 1:
+        groups = [list(range(size * p, size * p + size)) for p in range(PARTS)]
+        value = lax.psum_scatter(
+            value, ("cells", "rep"), scatter_dimension=0, axis_index_groups=groups, tiled=True
+        )
+    return value
+
+
+def group_sum(grid, values):
+    size = grid.n // PARTS
+    if size > 1:
+        groups = [list(range(size * p, size * p + size)) for p in range(PARTS)]
+        values = lax.psum(values, ("cells", "rep"), axis_index_groups=groups)
+    return values
 
 
 def shards(
@@ -420,81 +1188,62 @@
     bn_shift,
 ):
     cell_total = float(cells_x.shape[0] * grid.n)
-    latent_width = dec_w1.shape[0]
-    gene_count = cells_x.shape[1]
-    (nrm0, nrm1, nrm2, nrm3, inv, first_act, second_act, latent_draw, third_act, fourth_act, head_out, ggroup, offsets) = (
-        call_forward(
-            grid,
-            cells_x,
-            enc_w1.T,
-            latent_noise,
-            group_ids.reshape(1, -1),
-            owner_table,
-            owner_mask,
-            enc_w2,
-            head_w.T,
-            head_b.reshape(1, -1),
-            dec_w1,
-            dec_w2,
-            bn_gain,
-            bn_shift,
-        )
-    )
-    latent_mean = head_out[:, :latent_width]
-    logvar = head_out[:, latent_width:]
-    deviation = jnp.exp(0.5 * logvar)
-    member = (group_ids[:, None] == jnp.arange(ggroup.shape[0], dtype=jnp.int32)[None, :]).astype(F32)
-    grad_group = jnp.dot(member, ggroup, precision=lax.Precision.HIGHEST, preferred_element_type=F32)[:, :latent_width]
-    residual = (
-        jnp.dot(fourth_act, out_w, preferred_element_type=F32) + out_b - cells_x.astype(F32)
-    )
-    grad_recon = (residual * (2.0 / cell_total)).astype(BF16)
-    grad_out_w = contract_rows(fourth_act, grad_recon)
-    grad_out_b = jnp.sum(grad_recon.astype(F32), axis=0)
-    grad_fourth = contract_cols(grad_recon, out_w)
-    grad_pre4, gain_three, shift_three = norm_backward(grad_fourth, nrm3, inv[3], bn_gain[3], bn_shift[3], cell_total)
-    grad_dec_w2 = contract_rows(third_act, grad_pre4)
-    grad_third = contract_cols(grad_pre4, dec_w2)
-    grad_pre3, gain_two, shift_two = norm_backward(grad_third, nrm2, inv[2], bn_gain[2], bn_shift[2], cell_total)
-    grad_dec_w1 = contract_rows(latent_draw, grad_pre3)
-    grad_latent = contract_cols(grad_pre3, dec_w1)
-    kl_scale = KL_WEIGHT * gene_count / cell_total
-    grad_mean = grad_latent + kl_scale * latent_mean + grad_group
-    grad_logvar = grad_latent * latent_noise * (0.5 * deviation) + 0.5 * kl_scale * (jnp.exp(logvar) - 1.0)
-    grad_head = jnp.concatenate([grad_mean, grad_logvar], axis=1).astype(BF16)
-    grad_head_w = contract_rows(second_act, grad_head)
-    grad_head_b = jnp.sum(grad_head.astype(F32), axis=0)
-    grad_second = contract_cols(grad_head, head_w)
-    grad_pre2, gain_one, shift_one = norm_backward(grad_second, nrm1, inv[1], bn_gain[1], bn_shift[1], cell_total)
-    grad_enc_w2 = contract_rows(first_act, grad_pre2)
-    grad_first = contract_cols(grad_pre2, enc_w2)
-    grad_pre1, gain_zero, shift_zero = norm_backward(grad_first, nrm0, inv[0], bn_gain[0], bn_shift[0], cell_total)
-    grad_enc_w1 = contract_rows(cells_x, grad_pre1)
-    grad_x = cell_total * contract_cols(grad_pre1, enc_w1) - 2.0 * residual
-    summed_head_b, summed_out_b, summed_head_w, summed_dec_w1 = lax.psum(
-        (grad_head_b, grad_out_b, grad_head_w, grad_dec_w1), ("cells", "rep")
-    )
-    flat_out = grad_out_w.reshape(FLAT_ROWS, FLAT_COLS)
-    flat_enc = grad_enc_w1.reshape(FLAT_ROWS, FLAT_COLS)
-    flat_narrow = jnp.concatenate([grad_enc_w2.reshape(-1), grad_dec_w2.reshape(-1)]).reshape(
-        NARROW_ROWS, NARROW_COLS
-    )
-    shard_out, shard_enc, shard_narrow = (
-        lax.psum_scatter(flat_out, ("cells", "rep"), scatter_dimension=0, tiled=True),
-        lax.psum_scatter(flat_enc, ("cells", "rep"), scatter_dimension=0, tiled=True),
-        lax.psum_scatter(flat_narrow, ("cells", "rep"), scatter_dimension=0, tiled=True),
-    )
-    grad_gain = jnp.stack([gain_zero, gain_one, gain_two, gain_three])
-    grad_shift = jnp.stack([shift_zero, shift_one, shift_two, shift_three])
+    genes = cells_x.shape[1]
+    hidden = enc_w2.shape[0]
+    gid = group_ids.reshape(1, -1)
+    headt = head_w.T
+    *kept, offsets = call_forward(
+        grid,
+        cells_x,
+        enc_w1.T,
+        latent_noise,
+        gid,
+        owner_table,
+        owner_mask,
+        enc_w2,
+        headt,
+        head_b.reshape(1, -1),
+        dec_w1,
+        dec_w2,
+        bn_gain,
+        bn_shift,
+    )
+    g, gpre1, out25, enc_part, nar_part, d1_grad, headw_grad, outb_grad, headb_grad, grad_gain, grad_shift = call_backward(
+        grid,
+        kept,
+        cells_x,
+        out_w,
+        latent_noise,
+        gid,
+        out_b.reshape(1, -1),
+        enc_w2,
+        headt,
+        dec_w1,
+        dec_w2,
+        bn_gain,
+        bn_shift,
+    )
+    product = lax.dot_general(gpre1, enc_w1, (((1,), (1,)), ((), ())), preferred_element_type=F32)
+    grad_x = cell_total * (product - g[:, :genes].astype(F32))
+    part = grid.me() // (grid.n // PARTS)
+    each = genes * hidden // PARTS
+    enc_flat = lax.dynamic_slice_in_dim(enc_part.reshape(-1), (genes * part) % PARTS * (hidden // PARTS), each)
+    shard_enc = flat_shard(grid, enc_flat, FLAT_COLS, FLAT_ROWS)
+    shard_out = flat_shard(grid, out25[:, :genes], FLAT_COLS, FLAT_ROWS)
+    shard_narrow = flat_shard(grid, nar_part[: 2 * hidden // PARTS], NARROW_COLS, NARROW_ROWS)
+    headw_grad, d1_grad, headb_grad, outb_grad = group_sum(
+        grid,
+        (headw_grad.T, d1_grad, headb_grad.reshape(-1)[: head_b.shape[0]], outb_grad.reshape(-1)[:genes]),
+    )
     return (
         grad_x,
         shard_enc,
         shard_narrow,
-        summed_head_w,
-        summed_dec_w1,
-        summed_head_b,
+        headw_grad,
+        d1_grad,
+        headb_grad,
         shard_out,
-        summed_out_b,
+        outb_grad,
         grad_gain,
         grad_shift,
         offsets[None],

time: 1000 us -> 523 us (0.52)
  waiting for transfers between devices: 518 us -> 0 us
  Pallas kernels: 61.6 us -> 477 us
  blocking collectives: 161 us -> 0 us
  matrix products: 110 us -> 17.8 us
  local copies, waits for them, and re-layouts: 110 us -> 20.2 us
  other arithmetic: 16.5 us -> 0 us
  between operations: 14.4 us -> 1.16 us
    unnamed x6 -> x0, waiting for transfers between devices: 499 us -> none
    pallas_call x0 -> x1, Pallas kernels: none -> 416 us  [call_backward(): pl.pallas_call(functools.partial(backward_kernel, grid, latent), out_shap...]
    psum x4 -> x0, blocking collectives: 161 us -> none  [norm_backward(): lax.psum((jnp.sum(grad_pre, axis=0), jnp.sum(grad_pre * normed, axis=0)),...]
    dot_general x14 -> x1, matrix products: 110 us -> 17.8 us  [shards(): lax.dot_general(gpre1, enc_w1, (((1,), (1,)), ((), ())), preferred_elemen...]
    reshape x3 -> x6, local copies, waits for them, and re-layouts: 60.2 us -> 8.98 us  [the longest x3 4.61 us: flat_shard(): value = flat.reshape(rows_in_all // PARTS, columns)]
    dot_general x2 -> x0, local copies, waits for them, and re-layouts: 25.7 us -> none  [the longest x1 25.6 us: contract_rows(): lax.dot_general(left, right, (((0,), (0,)), ((), ())), preferred_element_...]
    reduce_scatter x1 -> x0, waiting for transfers between devices: 18.7 us -> none  [shards(): lax.psum_scatter(flat_narrow, ('cells', 'rep'), scatter_dimension=0, tile...]
    concatenate x2 -> x0, local copies, waits for them, and re-layouts: 10.7 us -> none  [shards(): jnp.concatenate([grad_enc_w2.reshape(-1), grad_dec_w2.reshape(-1)])]
  transfers between devices with their start and end apart: 4 -> 0, of which waited for: 3 -> 0; matrix products, arithmetic and copies ran while one was open for 17% -> 0% of each run, Pallas kernels for 0% -> 0%
where the time goes in v2:
time: 523 us; the launch traced here: 516 us
  Pallas kernels  477 us (91%)
  local copies, waits for them, and re-layouts  20.2 us (4%)
  matrix products  17.8 us (3%)
    pallas_call x1, Pallas kernels, call_backward(): pl.pallas_call(functools.partial(backward_kernel, grid, latent), out_shap...  416 us
    pallas_call x1, Pallas kernels, call_forward(): pl.pallas_call(functools.partial(forward_kernel, grid), out_shape=out_sha...  61.5 us
    dot_general x1, matrix products, shards(): lax.dot_general(gpre1, enc_w1, (((1,), (1,)), ((), ())), preferred_elemen...  17.8 us

profile of v2, /device:TPU:0, one launch (start us, length us, event | category | flops | bytes accessed | tf_op | source)
XLA Modules:
  0.0 516.2 jit_solution(17297770662123345795)
XLA Ops:
  0.7 1.3 reshape.49.gid_ref
  1.9 1.4 copy.26.table_ref
  3.3 1.4 copy.27.mask_ref
  4.6 1.4 reshape.51.outb_ref
  6.0 1.8 copy.28.noise_ref
  7.8 61.5 %forward.1 = (f32[576,800]{1,0:T(8,128)}, f32[576,800]{1,0:T(8,128)}, f32[576,800]{1,0:T(8,128)}, f32[576,800]{1,0:T(8,128)}, f32[4,800]{1,0:T(4,128)}, /*index=...) custom-call(s32[16,4]{1,0:T(8,128)} %copy.26.table_ref, ...), custom_call_target="tpu_custom_call" | custom-call | tf_op jit(solution)/shard_map/forward/pallas_call | solution.py:372
  69.3 415.5 %backward.1 = (bf16[576,7168]{1,0:T(8,128)(2,1)}, bf16[576,800]{1,0:T(8,128)(2,1)}, f32[25,7168]{1,0:T(8,128)}, f32[224,800]{1,0:T(8,128)}, f32[56,800]{1,0:T(8,...) custom-call(bf16[576,7000]{1,0:T(8,128)(2,1)} %x_hbm.3, ...), custom_call_target="tpu_custom_call" | custom-call | tf_op jit(solution)/shard_map/backward/pallas_call | solution.py:1116
  484.9 1.2 slice.17
  486.1 1.8 reshape.54
  487.9 1.7 reshape.52
  489.7 0.3 dynamic_slice.3
  489.9 1.5 reshape.53
  491.4 1.2 slice.18
  492.6 1.3 reshape.56
  494.0 0.0 copy-start
  494.0 0.0 copy-start.1
  494.0 0.0 copy-start.2
  494.0 0.0 copy-start.4
  494.0 0.0 copy-start.3
  494.0 0.0 copy-start.5
  494.0 17.8 %subtract_multiply_fusion = f32[576,7000]{1,0:T(8,128)} fusion(bf16[576,800]{1,0:T(8,128)(2,1)} %get-tuple-element.47, bf16[7000,800]{0,1:T(8,128)(2,1)} %param.20, bf16[576,7168]{1,0:T(8,128)(2,1)} %get-tuple-element.48), kind=kOutput, calls=%fused_computation | convolution fusion | flops 6463296000 | bytes 36313600 | tf_op jit(solution)/shard_map/dot_general | solution.py:1226
  511.8 0.0 copy-done
  511.8 0.9 copy.36
  512.6 0.0 copy-done.1
  512.6 0.7 copy.37
  513.4 0.0 copy-done.2
  513.4 0.6 copy.38
  514.0 0.0 copy-done.4
  514.0 0.6 copy.39
  514.6 0.0 copy-done.3
  514.6 0.6 copy.40
  515.2 0.0 copy-done.5
  515.2 0.6 copy.41
Async XLA Ops:
  494.0 17.8 %copy-start = (f32[200,800]{1,0:T(8,128)S(1)}, f32[200,800]{1,0:T(8,128)}, u32[]{:S(2)}) copy-start(f32[200,800]{1,0:T(8,128)} %get-tuple-element.51) | copy-start | bytes 1920004
  494.0 18.7 %copy-start.1 = (f32[100,800]{1,0:T(8,128)S(1)}, f32[100,800]{1,0:T(8,128)}, u32[]{:S(2)}) copy-start(f32[100,800]{1,0:T(8,128)} %get-tuple-element.74) | copy-start | bytes 960004
  494.0 19.4 %copy-start.2 = (f32[56,128]{1,0:T(8,128)S(1)}, f32[56,128]{1,0:T(8,128)}, u32[]{:S(2)}) copy-start(f32[56,128]{1,0:T(8,128)} %get-tuple-element.55) | copy-start | bytes 86020
  494.0 20.0 %copy-start.4 = (f32[4,800]{1,0:T(4,128)S(1)}, f32[4,800]{1,0:T(4,128)}, u32[]{:S(2)}) copy-start(f32[4,800]{1,0:T(4,128)} %get-tuple-element.78) | copy-start | bytes 38404
  494.0 20.6 %copy-start.3 = (f32[4,800]{1,0:T(4,128)S(1)}, f32[4,800]{1,0:T(4,128)}, u32[]{:S(2)}) copy-start(f32[4,800]{1,0:T(4,128)} %get-tuple-element.79) | copy-start | bytes 38404
  494.0 21.2 %copy-start.5 = (f32[4,100]{1,0:T(4,128)S(1)}, f32[4,100]{1,0:T(4,128)}, u32[]{:S(2)}) copy-start(f32[4,100]{1,0:T(4,128)} %get-tuple-element.58) | copy-start | bytes 4804

commit v3 on v2

--- a/solution.py
+++ b/solution.py
@@ -128,7 +128,10 @@
     return jnp.sum(value, axis=0, keepdims=True)
 
 
-def batch_norm(pre, nrm_out, act_out, gather, slot, gain_row, shift_row, inv_out):
+PARTS = 32
+
+
+def batch_norm(pre, nrm_out, act_out, gather, slot, gain_row, shift_row, inv_out, idle):
     rows, width = pre.shape
     total = row_loop(rows, lambda r, c: c + column_sum(pre[r, :]), jnp.zeros((1, width), F32))
     mean = total * (1.0 / rows)
@@ -146,6 +149,7 @@
     for level in range(levels):
         size = gather.grid.digits[level][1]
         gather.start(level, slot)
+        idle()
         gather.wait(level, slot)
         buffer = gather.buffers[level].at[slot]
         means = [buffer[g, 0:8, :] for g in range(size)]
@@ -226,9 +230,10 @@
     act4,
     head_out,
     ggroup_out,
+    xt_out,
     offsets_out,
-    x_win,
-    x_tail,
+    x_all,
+    xt,
     w_win,
     w_tail,
     pre,
@@ -244,7 +249,7 @@
         rest[4 * levels : 5 * levels],
         rest[5 * levels : 6 * levels],
     )
-    in_sems = rest[6 * levels]
+    in_sems, xt_sems = rest[6 * levels :]
     gather = Gather(grid, small, s_send, s_recv)
     group_gather = Gather(grid, wide, g_send, g_recv)
     latent = d1_ref.shape[0]
@@ -253,7 +258,7 @@
 
     loads = []
     for i, (s, size) in enumerate(spans):
-        a = pltpu.make_async_copy(x_hbm.at[:, pl.ds(s, size)], part_of(x_win, x_tail, i), in_sems.at[0, i])
+        a = pltpu.make_async_copy(x_hbm.at[:, pl.ds(s, size)], x_all.at[:, pl.ds(s, size)], in_sems.at[0, i])
         b = pltpu.make_async_copy(w1_hbm.at[:, pl.ds(s, size)], part_of(w_win, w_tail, i), in_sems.at[1, i])
         a.start()
         b.start()
@@ -263,12 +268,37 @@
     for i, (s, size) in enumerate(spans):
         loads[i][0].wait()
         loads[i][1].wait()
-        part = nt(part_of(x_win, x_tail, i)[...], part_of(w_win, w_tail, i)[...])
+        part = nt(x_all[:, s : s + size], part_of(w_win, w_tail, i)[...])
         pre[...] = part if i == 0 else pre[...] + part
+
+    starts = [(genes * j) // PARTS for j in range(PARTS)]
+    parts_left = list(range(PARTS))
+
+    def save(j):
+        return pltpu.make_async_copy(xt.at[j], xt_out.at[j], xt_sems.at[j])
+
+    def transpose():
+        for j in parts_left[: -(-PARTS // (4 * levels))]:
+            at = starts[j] // 128 * 128
+            size = min(384, genes - at)
+            lane = lax.broadcasted_iota(jnp.int32, (xt.shape[1], size), 1)
+            line = lax.broadcasted_iota(jnp.int32, (xt.shape[1], size), 0)
+            select = jnp.where(lane == line + (starts[j] - at), 1.0, 0.0).astype(BF16)
+            xt[j] = nt(select, x_all[:, at : at + size]).astype(BF16)
+            save(j).start()
+            parts_left.remove(j)
 
     def norm(k, nrm, act):
         batch_norm(
-            pre, nrm, act, gather, k, gain_ref[k : k + 1, :], shift_ref[k : k + 1, :], inv_out.at[k : k + 1, :]
+            pre,
+            nrm,
+            act,
+            gather,
+            k,
+            gain_ref[k : k + 1, :],
+            shift_ref[k : k + 1, :],
+            inv_out.at[k : k + 1, :],
+            transpose,
         )
 
     norm(0, nrm0, act1)
@@ -319,6 +349,8 @@
     moments[even, :] = -grad_offset
     ggroup_out[...] = moments[...] / counted
 
+    for j in range(PARTS):
+        save(j).wait()
     for level in range(levels):
         for k in range(4):
             gather.finish(level, k)
@@ -350,12 +382,13 @@
         wide_b,
         jax.ShapeDtypeStruct((rows, 2 * latent), F32),
         jax.ShapeDtypeStruct((groups, 128), F32),
+        jax.ShapeDtypeStruct((PARTS, 32 * count, rows), BF16),
         jax.ShapeDtypeStruct((table.shape[1], latent), F32),
     )
     scratch = (
         [
-            pltpu.VMEM((count - 1, rows, WIN), BF16),
-            pltpu.VMEM((rows, genes - (count - 1) * WIN), BF16),
+            pltpu.VMEM((rows, genes), BF16),
+            pltpu.VMEM((PARTS, 32 * count, rows), BF16),
             pltpu.VMEM((count - 1, hidden, WIN), BF16),
             pltpu.VMEM((hidden, genes - (count - 1) * WIN), BF16),
             pltpu.VMEM((rows, hidden), F32),
@@ -367,13 +400,13 @@
         + [pltpu.SemaphoreType.DMA((4, size - 1)) for _, size in grid.digits]
         + [pltpu.SemaphoreType.DMA((1, size - 1)) for _, size in grid.digits]
         + [pltpu.SemaphoreType.DMA((1, size - 1)) for _, size in grid.digits]
-        + [pltpu.SemaphoreType.DMA((2, count))]
+        + [pltpu.SemaphoreType.DMA((2, count)), pltpu.SemaphoreType.DMA((PARTS,))]
     )
     return pl.pallas_call(
         functools.partial(forward_kernel, grid),
         out_shape=out_shape,
         in_specs=[sm, sm, hbm, hbm] + [vm] * 9,
-        out_specs=[vm] * len(out_shape),
+        out_specs=[vm] * (len(out_shape) - 2) + [hbm, vm],
         scratch_shapes=scratch,
         name="forward",
         compiler_params=pltpu.CompilerParams(
@@ -382,9 +415,320 @@
     )(table, mask, cells_x, w1t, noise, gid, w2, headt, headb, d1, d2, gain, shift)
 
 
-ORDERS = ((0, 1, 2, 3, 4), (0, 2, 1, 3, 4), (0, 1, 3, 4, 2), (0, 2, 3, 4, 1))
-CHANNELS = len(ORDERS)
-PARTS = 32
+ORDERS = (
+    (0, 2, 3, 4, 1),
+    (0, 3, 1, 2, 4),
+    (0, 2, 3, 1, 4),
+    (0, 1, 3, 2, 4),
+    (0, 2, 3, 1, 4),
+    (0, 1, 2, 3, 4),
+    (0, 2, 1, 3, 4),
+    (0, 1, 2, 3, 4),
+    (0, 2, 1, 3, 4),
+    (0, 3, 1, 2, 4),
+    (0, 1, 3, 2, 4),
+    (0, 2, 3, 1, 4),
+    (0, 1, 3, 2, 4),
+    (0, 2, 1, 3, 4),
+    (0, 2, 3, 1, 4),
+    (0, 1, 2, 3, 4),
+)
+C, U, L, S, F = range(5)
+PLAN = (
+    (C,),
+    (U, 0),
+    (C,),
+    (C,),
+    (L, 0),
+    (S, 0, 1, 0, 1),
+    (S, 0, 1, 1, 2),
+    (U, 1),
+    (S, 0, 1, 3, 1),
+    (C,),
+    (S, 0, 1, 4, 1),
+    (C,),
+    (L, 1),
+    (S, 1, 1, 0, 1),
+    (S, 0, 1, 5, 1),
+    (S, 1, 1, 1, 1),
+    (C,),
+    (S, 0, 1, 6, 1),
+    (S, 1, 1, 2, 1),
+    (C,),
+    (S, 1, 1, 3, 1),
+    (C,),
+    (S, 0, 1, 7, 1),
+    (S, 1, 1, 4, 1),
+    (C,),
+    (C,),
+    (S, 1, 1, 5, 2),
+    (U, 2),
+    (F, 0, 1),
+    (S, 1, 1, 7, 1),
+    (C,),
+    (S, 0, 2, 0, 1),
+    (C,),
+    (L, 2),
+    (S, 2, 1, 0, 1),
+    (S, 2, 1, 1, 2),
+    (S, 0, 2, 1, 2),
+    (U, 3),
+    (F, 1, 1),
+    (S, 1, 2, 0, 1),
+    (S, 1, 2, 1, 1),
+    (S, 2, 1, 3, 2),
+    (S, 0, 2, 3, 1),
+    (C,),
+    (S, 1, 2, 2, 1),
+    (C,),
+    (L, 3),
+    (C,),
+    (C,),
+    (S, 1, 2, 3, 1),
+    (S, 3, 1, 0, 1),
+    (S, 2, 1, 5, 2),
+    (F, 0, 2),
+    (S, 0, 3, 0, 1),
+    (S, 3, 1, 1, 2),
+    (S, 2, 1, 7, 1),
+    (S, 0, 3, 1, 1),
+    (U, 4),
+    (C,),
+    (S, 3, 1, 3, 1),
+    (F, 1, 2),
+    (S, 1, 3, 0, 1),
+    (F, 2, 1),
+    (S, 1, 3, 1, 1),
+    (S, 2, 2, 0, 1),
+    (L, 4),
+    (S, 3, 1, 4, 2),
+    (S, 4, 1, 0, 2),
+    (S, 2, 2, 1, 2),
+    (U, 5),
+    (F, 0, 3),
+    (F, 1, 3),
+    (S, 3, 1, 6, 2),
+    (S, 4, 1, 2, 2),
+    (S, 2, 2, 3, 1),
+    (S, 1, 4, 0, 1),
+    (C,),
+    (L, 5),
+    (C,),
+    (C,),
+    (S, 0, 4, 0, 1),
+    (S, 5, 1, 0, 1),
+    (S, 4, 1, 4, 2),
+    (F, 2, 2),
+    (S, 5, 1, 1, 2),
+    (S, 4, 1, 6, 2),
+    (U, 6),
+    (C,),
+    (S, 5, 1, 3, 1),
+    (F, 0, 4),
+    (F, 1, 4),
+    (F, 3, 1),
+    (S, 3, 2, 0, 1),
+    (S, 3, 2, 1, 1),
+    (L, 6),
+    (S, 6, 1, 0, 1),
+    (S, 5, 1, 4, 2),
+    (S, 6, 1, 1, 2),
+    (S, 3, 2, 2, 2),
+    (C,),
+    (F, 4, 1),
+    (C,),
+    (C,),
+    (S, 5, 1, 6, 2),
+    (S, 6, 1, 3, 2),
+    (S, 4, 2, 0, 2),
+    (F, 3, 2),
+    (C,),
+    (S, 2, 3, 0, 2),
+    (S, 6, 1, 5, 2),
+    (S, 4, 2, 2, 2),
+    (F, 5, 1),
+    (S, 6, 1, 7, 1),
+    (S, 3, 3, 0, 1),
+    (C,),
+    (F, 2, 3),
+    (S, 2, 4, 0, 1),
+    (F, 4, 2),
+    (S, 4, 3, 0, 1),
+    (C,),
+    (C,),
+    (S, 4, 3, 1, 1),
+    (S, 3, 3, 1, 1),
+    (S, 5, 2, 0, 1),
+    (F, 6, 1),
+    (S, 6, 2, 0, 1),
+    (F, 2, 4),
+    (C,),
+    (S, 6, 2, 1, 2),
+    (S, 5, 2, 1, 2),
+    (F, 3, 3),
+    (S, 3, 4, 0, 1),
+    (F, 4, 3),
+    (S, 6, 2, 3, 1),
+    (S, 5, 2, 3, 1),
+    (S, 4, 4, 0, 1),
+    (C,),
+    (F, 3, 4),
+    (U, 7),
+    (F, 5, 2),
+    (S, 5, 3, 0, 2),
+    (F, 6, 2),
+    (S, 6, 3, 0, 2),
+    (F, 4, 4),
+    (L, 7),
+    (S, 7, 1, 0, 2),
+    (S, 7, 1, 2, 2),
+    (S, 7, 1, 4, 2),
+    (U, 8),
+    (F, 5, 3),
+    (S, 7, 1, 6, 1),
+    (S, 5, 4, 0, 1),
+    (L, 8),
+    (S, 7, 1, 7, 1),
+    (S, 8, 1, 0, 2),
+    (S, 8, 1, 2, 2),
+    (S, 8, 1, 4, 2),
+    (S, 8, 1, 6, 2),
+    (U, 9),
+    (F, 6, 3),
+    (S, 6, 4, 0, 1),
+    (F, 5, 4),
+    (L, 9),
+    (S, 9, 1, 0, 2),
+    (S, 9, 1, 2, 2),
+    (S, 9, 1, 4, 1),
+    (U, 10),
+    (S, 9, 1, 5, 1),
+    (F, 6, 4),
+    (S, 9, 1, 6, 1),
+    (L, 10),
+    (S, 10, 1, 0, 2),
+    (S, 10, 1, 2, 2),
+    (S, 10, 1, 4, 2),
+    (S, 9, 1, 7, 1),
+    (F, 7, 1),
+    (S, 10, 1, 6, 1),
+    (S, 7, 2, 0, 2),
+    (S, 7, 2, 2, 2),
+    (F, 8, 1),
+    (U, 11),
+    (S, 10, 1, 7, 1),
+    (S, 8, 2, 0, 1),
+    (L, 11),
+    (S, 8, 2, 1, 1),
+    (U, 12),
+    (S, 8, 2, 2, 2),
+    (F, 7, 2),
+    (S, 7, 3, 0, 2),
+    (S, 11, 1, 0, 2),
+    (S, 11, 1, 2, 2),
+    (S, 11, 1, 4, 2),
+    (L, 12),
+    (F, 9, 1),
+    (S, 9, 2, 0, 2),
+    (S, 11, 1, 6, 1),
+    (U, 13),
+    (F, 10, 1),
+    (S, 9, 2, 2, 2),
+    (S, 11, 1, 7, 1),
+    (S, 10, 2, 0, 2),
+    (S, 10, 2, 2, 2),
+    (F, 7, 3),
+    (S, 7, 4, 0, 1),
+    (L, 13),
+    (U, 14),
+    (F, 8, 2),
+    (S, 8, 3, 0, 2),
+    (S, 12, 1, 0, 2),
+    (S, 12, 1, 2, 1),
+    (L, 14),
+    (S, 12, 1, 3, 1),
+    (F, 10, 2),
+    (S, 10, 3, 0, 2),
+    (S, 12, 1, 4, 1),
+    (S, 14, 1, 0, 2),
+    (S, 14, 1, 2, 2),
+    (F, 11, 1),
+    (S, 12, 1, 5, 1),
+    (S, 14, 1, 4, 1),
+    (S, 11, 2, 0, 2),
+    (S, 11, 2, 2, 2),
+    (U, 15),
+    (F, 7, 4),
+    (S, 12, 1, 6, 1),
+    (S, 14, 1, 5, 1),
+    (F, 9, 2),
+    (F, 10, 3),
+    (S, 14, 1, 6, 1),
+    (S, 10, 4, 0, 1),
+    (S, 12, 1, 7, 1),
+    (F, 8, 3),
+    (S, 8, 4, 0, 1),
+    (L, 15),
+    (S, 14, 1, 7, 1),
+    (F, 11, 2),
+    (S, 11, 3, 0, 2),
+    (S, 9, 3, 0, 2),
+    (S, 13, 1, 0, 1),
+    (S, 15, 1, 0, 2),
+    (F, 10, 4),
+    (S, 15, 1, 2, 2),
+    (S, 13, 1, 1, 2),
+    (F, 12, 1),
+    (S, 15, 1, 4, 1),
+    (S, 13, 1, 3, 1),
+    (S, 12, 2, 0, 2),
+    (S, 12, 2, 2, 2),
+    (F, 8, 4),
+    (F, 14, 1),
+    (S, 15, 1, 5, 1),
+    (S, 13, 1, 4, 1),
+    (S, 14, 2, 0, 2),
+    (S, 14, 2, 2, 1),
+    (F, 11, 3),
+    (S, 15, 1, 6, 1),
+    (S, 13, 1, 5, 1),
+    (S, 14, 2, 3, 1),
+    (F, 9, 3),
+    (S, 13, 1, 6, 1),
+    (S, 9, 4, 0, 1),
+    (S, 15, 1, 7, 1),
+    (F, 12, 2),
+    (S, 13, 1, 7, 1),
+    (S, 11, 4, 0, 1),
+    (F, 14, 2),
+    (S, 14, 3, 0, 2),
+    (S, 12, 3, 0, 2),
+    (F, 15, 1),
+    (S, 15, 2, 0, 2),
+    (S, 15, 2, 2, 2),
+    (F, 9, 4),
+    (F, 13, 1),
+    (S, 13, 2, 0, 2),
+    (S, 13, 2, 2, 2),
+    (F, 14, 3),
+    (S, 14, 4, 0, 1),
+    (F, 11, 4),
+    (F, 12, 3),
+    (S, 12, 4, 0, 1),
+    (F, 14, 4),
+    (F, 13, 2),
+    (S, 13, 3, 0, 2),
+    (F, 12, 4),
+    (F, 15, 2),
+    (S, 15, 3, 0, 2),
+    (F, 13, 3),
+    (S, 13, 4, 0, 1),
+    (F, 15, 3),
+    (S, 15, 4, 0, 1),
+    (F, 13, 4),
+    (F, 15, 4),
+)
+CHANNELS = 4
 STAGES = 5
 SLOT_ROWS = 200
 
@@ -403,41 +747,42 @@
     def partner(self, b):
         return self.grid.place(self.grid.me() + (1 - 2 * self.bit(b)) * (1 << (b + self.shift)))
 
-    def part(self, channel, k):
+    def part(self, q, k):
         out = 0
-        for t, b in enumerate(ORDERS[channel]):
+        for t, b in enumerate(ORDERS[q]):
             own = self.bit(b)
             out = out + (1 << b) * ((1 - own) if (k >> (STAGES - 1 - t)) & 1 else own)
         return out
 
-    def send(self, q, t):
+    def send(self, q, t, first=0, number=None):
         channel, rows = q % CHANNELS, self.rows[q]
-        size = (16 >> t) * rows
+        slots = 16 >> t
+        at, size = first * rows, (slots if number is None else number) * rows
         if t == 0:
-            source, sem = self.stage.at[q % 2, 0:size], self.stage_sems.at[q % 2]
+            source, sem = self.stage.at[q % 2, at : at + size], self.stage_sems.at[q % 2]
         else:
-            source, sem = self.landing[t - 1].at[channel, size : 2 * size], self.send_sems.at[channel, t]
+            start = slots * rows + at
+            source, sem = self.landing[t - 1].at[channel, start : start + size], self.send_sems.at[channel, t]
         return pltpu.make_async_remote_copy(
             src_ref=source,
-            dst_ref=self.landing[t].at[channel, 0:size],
+            dst_ref=self.landing[t].at[channel, at : at + size],
             send_sem=sem,
             recv_sem=self.recv_sems.at[channel, t],
-            device_id=self.partner(ORDERS[channel][t]),
+            device_id=self.partner(ORDERS[q][t]),
             device_id_type=MESH_ID,
         )
 
-    def start(self, q, t):
-        if q >= CHANNELS:
-            pl.semaphore_wait(self.credits.at[q % CHANNELS, t], 1)
-        self.send(q, t).start()
+    def feed(self, q, t, first, number):
+        if first == 0 and q >= CHANNELS:
+            pl.semaphore_wait(self.credits.at[q - CHANNELS, t], 1)
+        self.send(q, t, first, number).start()
 
     def free(self, q, t):
         if q + CHANNELS < self.total:
-            channel = q % CHANNELS
             pl.semaphore_signal(
-                self.credits.at[channel, t],
+                self.credits.at[q, t],
                 inc=1,
-                device_id=self.partner(ORDERS[channel][t]),
+                device_id=self.partner(ORDERS[q + CHANNELS][t]),
                 device_id_type=MESH_ID,
             )
 
@@ -446,11 +791,11 @@
         if q >= 2:
             self.send(q - 2, 0).wait_send()
         fill(self.stage.at[q % 2], True)
-        self.start(q, 0)
-
-    def lower(self, q, fill):
+        self.feed(q, 0, 0, 16)
+        fill(self.low, False)
+
+    def lower(self, q):
         channel, rows = q % CHANNELS, self.rows[q]
-        fill(self.low, False)
         self.send(q, 0).wait_recv()
         mine = self.landing[0].at[channel]
 
@@ -460,7 +805,6 @@
             return c
 
         lax.fori_loop(0, 16, add, 0)
-        self.start(q, 1)
 
     def fold(self, q, t):
         channel, rows = q % CHANNELS, self.rows[q]
@@ -475,7 +819,6 @@
         lax.fori_loop(0, 16 >> t, add, 0)
         self.send(q, t).wait_send()
         self.free(q, t - 1)
-        self.start(q, t + 1)
 
     def last(self, q, done):
         channel, rows = q % CHANNELS, self.rows[q]
@@ -559,8 +902,8 @@
     return column, part
 
 
-def slot_of(scatter, channel, bits, parts, part):
-    order = [b for b in ORDERS[channel] if b in bits]
+def slot_of(scatter, q, bits, parts, part):
+    order = [b for b in ORDERS[q] if b in bits]
     slot = jnp.zeros_like(part)
     for value in range(parts):
         at = 0
@@ -572,12 +915,13 @@
     return slot
 
 
-def sum_blocks(gather, slot, idle):
+def sum_blocks(gather, slot):
     levels = len(gather.grid.digits)
+    yield
     for level in range(levels):
         gather.start(level, slot)
-        if level < len(idle):
-            idle[level]()
+        if level < 2:
+            yield
         gather.wait(level, slot)
         size = gather.grid.digits[level][1]
         buffer = gather.buffers[level].at[slot]
@@ -587,7 +931,7 @@
     return total
 
 
-def norm_gradient(grad, nrm, out, gather, slot, gain_row, shift_row, inv_row, scale, gain_out, shift_out, idle):
+def norm_gradient(grad, nrm, out, gather, slot, gain_row, shift_row, inv_row, scale, gain_out, shift_out):
     rows, width = grad.shape
 
     def gate(r, carry):
@@ -603,7 +947,7 @@
     own = gather.own(0, slot)
     put_row(own, 0, shift_sum, width)
     put_row(own, 8, gain_sum, width)
-    total = sum_blocks(gather, slot, idle)
+    total = yield from sum_blocks(gather, slot)
     shift_sum = take_row(total, 0, width)
     gain_sum = take_row(total, 8, width)
     shift_out[...] = shift_sum
@@ -635,6 +979,7 @@
     act1_hbm,
     act2_hbm,
     act3_hbm,
+    xt_hbm,
     act4_ref,
     zlat_ref,
     head_ref_in,
@@ -677,7 +1022,7 @@
     (rep_sems,) = take(1)
     g_win, wide, gact, gpre4, gpre3, gpre2, ghead, gcell, lhs, nrm_buf, fin = take(11)
     picked = lhs.at[0:512]
-    in_sems, g_sems, nrm_sems, x_sems, act_sems = take(5)
+    in_sems, g_sems, nrm_sems, xt_sem, act_sems = take(5)
 
     rows, genes = x_hbm.shape
     hidden = w2_ref.shape[0]
@@ -686,6 +1031,7 @@
     cell_total = float(rows * grid.n)
     total = 2 * count + 2
     gather = Gather(grid, small, s_send, s_recv)
+    first = count
     scatter = Scatter(grid, total, stage, low, landing, stage_sems, send_sems, recv_sems, credits)
     spread = Spread(scatter, rep_block, rep_landing, rep_whole, rep_sems)
     rep_outb = 7 * (D1_ROWS + 2 * latent)
@@ -713,7 +1059,7 @@
 
     def out_lhs(q):
         column, part = column_parts(hidden, hidden // PARTS)
-        slot = slot_of(scatter, q % CHANNELS, (0, 1, 2, 3, 4), PARTS, part)
+        slot = slot_of(scatter, q, (0, 1, 2, 3, 4), PARTS, part)
         target = column + (hidden // PARTS) * (slot - part)
         block = hidden // 5
 
@@ -723,33 +1069,6 @@
             return c
 
         lax.fori_loop(0, 5, some, 0)
-
-    def out_piece(s):
-        out_lhs(s)
-        made(s, SLOT_ROWS, out_fill(s))
-
-    done = {}
-    state = {}
-
-    def reach(q, t):
-        while q in state and state[q] <= t:
-            stage_now = state[q]
-            if stage_now < STAGES - 1:
-                reach(q - CHANNELS, min(stage_now + 2, STAGES - 1))
-                scatter.fold(q, stage_now)
-            else:
-                scatter.last(q, done[q])
-            state[q] = stage_now + 1
-
-    def fold(q, t):
-        reach(q, t)
-
-    def made(q, rows_here, fill):
-        reach(q - CHANNELS, 1)
-        scatter.upper(q, rows_here, fill)
-        reach(q - CHANNELS, 2)
-        scatter.lower(q, fill)
-        state[q] = 1
 
     def out_done(s):
         def done(value):
@@ -759,8 +1078,34 @@
 
         return done
 
+    done = {s: out_done(s) for s in range(count)}
+    pieces = {}
     for s in range(count):
-        done[s] = out_done(s)
+        pieces[s] = (SLOT_ROWS, out_fill(s))
+
+    plan = list(PLAN)
+
+    def run(chain, more=None):
+        while plan:
+            what, *which = plan[0]
+            if what == C:
+                if next(chain, None) is None:
+                    return
+            elif what == U:
+                if which[0] < count:
+                    out_lhs(which[0])
+                scatter.upper(which[0], *pieces[which[0]])
+            elif what == L:
+                scatter.lower(which[0])
+            elif what == S:
+                scatter.feed(*which)
+            elif which[1] < STAGES - 1:
+                scatter.fold(*which)
+            else:
+                scatter.last(which[0], done[which[0]])
+            del plan[0]
+            if more is not None:
+                more()
 
     def output_layer(w_ring, w_tail, x_ring, x_tail):
         def load(s):
@@ -778,10 +1123,15 @@
         def save(s):
             return pltpu.make_async_copy(g_win.at[s % 3], g_out.at[:, pl.ds(WIN * s, WIN)], g_sems.at[s])
 
-        for s in range(2):
-            for copy in load(s):
-                copy.start()
-        for s, (at, size) in enumerate(spans):
+        def layers():
+            for s in range(2):
+                for copy in load(s):
+                    copy.start()
+            for s in range(count):
+                yield from layer(s)
+
+        def layer(s):
+            at, size = spans[s]
             tail = s == count - 1
             w = w_tail if tail else w_ring.at[s % 3]
             x = x_tail if tail else x_ring.at[s % 2]
@@ -806,12 +1156,12 @@
             if s + 2 < count:
                 for copy in load(s + 2):
                     copy.start()
-            if s < CHANNELS:
-                out_piece(s)
+            yield 0
             part = nt(g[:, 0:size], w[...])
             gact[...] = part if s == 0 else gact[...] + part
-            if s == count - 2:
-                fold(0, 1)
+            yield 0
+
+        run(layers())
         for s in range(count - 3, count):
             save(s).wait()
 
@@ -846,42 +1196,14 @@
                 height * full : height * full + 8, rest_width * i : rest_width * (i + 1)
             ]
 
-    def finish(xt, x_part, x_last, act_buf):
-        window = x_part.shape[2]
-        height = xt.shape[1]
-        starts = [(genes * j) // PARTS for j in range(PARTS)]
-
-        def x_place(j):
-            at = starts[j] // 128 * 128
-            return (at, window) if at + window <= genes else (at, genes - at)
-
-        def x_load(j):
-            at, size = x_place(j)
-            target = x_part.at[j % 3] if size == window else x_last
-            return pltpu.make_async_copy(x_hbm.at[:, pl.ds(at, size)], target, x_sems.at[j])
-
-        def transpose(j):
-            x_load(j).wait()
-            at, size = x_place(j)
-            source = x_part.at[j % 3] if size == window else x_last
-            lane = lax.broadcasted_iota(jnp.int32, (height, size), 1)
-            line = lax.broadcasted_iota(jnp.int32, (height, size), 0)
-            select = jnp.where(lane == line + (starts[j] - at), 1.0, 0.0).astype(BF16)
-            xt[j] = nt(select, source[...]).astype(BF16)
-            if j + 3 < PARTS:
-                x_load(j + 3).start()
-
-        def transposes(first, number):
-            def run():
-                for j in range(first, first + number):
-                    transpose(j)
-
-            return run
+    def finish(xt, act_buf):
+        xt_load = pltpu.make_async_copy(xt_hbm, xt, xt_sem)
+        xt_load.start()
 
         def enc_fill(q, s):
             def fill(target, is_upper):
                 for i in range(16):
-                    j = scatter.part(q % CHANNELS, 16 + i if is_upper else i)
+                    j = scatter.part(q, 16 + i if is_upper else i)
                     picked[32 * i : 32 * i + 32, :] = xt[j, 32 * s : 32 * s + 32, :]
                 wide[0:512, 0:hidden] = nn(picked[...], gpre1[...])
 
@@ -893,9 +1215,6 @@
 
             return fill
 
-        def enc_piece(q, s):
-            made(q, SLOT_ROWS, enc_fill(q, s))
-
         def enc_done(s):
             return lambda value: unpack(value, enc_part, 32 * s, 32)
 
@@ -905,12 +1224,11 @@
         def nar_fill(q, which):
             height_here = 32 if which == 0 else 24
             rows_here = 25 * 8 if which == 0 else 19 * 8
-            channel = q % CHANNELS
-            place = STAGES - 1 - ORDERS[channel].index(4)
+            place = STAGES - 1 - ORDERS[q].index(4)
 
             def fill(target, is_upper):
                 column, part = column_parts(hidden, each)
-                slot = slot_of(scatter, channel, (0, 1, 2, 3), PARTS // 2, part)
+                slot = slot_of(scatter, q, (0, 1, 2, 3), PARTS // 2, part)
                 line = column - each * part - skip[which]
                 inside = (line >= 0) & (line < height_here)
                 base = 8 if is_upper else 0
@@ -928,27 +1246,24 @@
 
             return rows_here, fill
 
-        def nar_piece(q, which):
-            rows_here, fill = nar_fill(q, which)
-            made(q, rows_here, fill)
-
         def nar_done(which):
             if which == 0:
                 return lambda value: unpack(value, nar_part, 0, 32)
             return lambda value: unpack(value, nar_part, 32, 24)
 
-        first = count
-        done[first] = nar_done(0)
-        done[first + 1] = nar_done(1)
+        for which in range(2):
+            done[first + which] = nar_done(which)
+            pieces[first + which] = nar_fill(first + which, which)
         for s in range(count):
             done[first + 2 + s] = enc_done(s)
+            pieces[first + 2 + s] = (SLOT_ROWS, enc_fill(first + 2 + s, s))
 
         def row(ref, k):
             return ref[k : k + 1, :]
 
-        def back(k, grad, out, idle):
+        def back(k, grad, out):
             nrm_loads[k].wait()
-            norm_gradient(
+            return norm_gradient(
                 grad,
                 nrm_buf.at[(k + 1) % 2],
                 out,
@@ -960,7 +1275,6 @@
                 1.0 / cell_total,
                 gain_out.at[k : k + 1, :],
                 shift_out.at[k : k + 1, :],
-                idle,
             )
 
         act_loads = [
@@ -969,31 +1283,6 @@
         ]
         act_loads[1].start()
         act_loads[2].start()
-        for j in range(3):
-            x_load(j).start()
-
-        groups = ggroup_ref.shape[0]
-        member = (lax.broadcasted_iota(jnp.int32, (groups, rows), 0) == gid_ref[...]).astype(F32)
-        gcell[...] = exact(member, ggroup_ref[...], ((0,), (0,)))
-
-        back(3, gact, gpre4, [transposes(0, 4), transposes(4, 4)])
-        nrm_loads[1].start()
-        gact[...] = nt(gpre4[...], d2_ref[...])
-        fold(1, 1)
-        back(2, gact, gpre3, [transposes(8, 4), transposes(12, 4)])
-        nrm_loads[0].start()
-        grad_z = nt(gpre3[...], d1_ref[...])
-        mu = head_ref_in[:, 0:latent]
-        logvar = head_ref_in[:, latent : 2 * latent]
-        kl = KL_WEIGHT * genes / cell_total
-        deviation = jnp.exp(0.5 * logvar)
-        grad_mu = grad_z + kl * mu + gcell[:, 0:latent]
-        grad_logvar = grad_z * noise_ref[...] * (0.5 * deviation) + 0.5 * kl * (jnp.exp(logvar) - 1.0)
-        ghead[...] = jnp.concatenate([grad_mu, grad_logvar], axis=1).astype(BF16)
-        gact[...] = nn(ghead[...], head_ref[...])
-        fold(0, 2)
-        out_piece(4)
-        fold(2, 1)
 
         def latent_side():
             act_loads[2].wait()
@@ -1007,39 +1296,49 @@
                 at = 7 * D1_ROWS + 2 * latent * c
                 rep_block[at : at + 2 * latent, 0:size] = headw_grad[:, 128 * c : 128 * c + size]
             put_row(rep_block, rep_headb, column_sum(ghead[...].astype(F32)), 2 * latent)
-            spread.step(0)
-
-        back(1, gact, gpre2, [transposes(16, 4), transposes(20, 4)])
-        gact[...] = nt(gpre2[...], w2_ref[...])
-        latent_side()
-        fold(1, 2)
-        out_piece(5)
-        fold(3, 1)
-        back(0, gact, gpre1, [transposes(24, 4), transposes(28, 4)])
-        fold(0, 3)
-        fold(2, 2)
-        out_piece(6)
-        for copy in act_loads[:2]:
-            copy.wait()
-
-        steps = list(range(1, 2 * STAGES + 1))
-        for q in range(count, total):
-            if q < first + 2:
-                nar_piece(q, q - first)
-            else:
-                enc_piece(q, q - first - 2)
-            for lag, t in ((3, 1), (4, 2), (5, 3), (6, 4)):
-                if q - lag >= 0:
-                    fold(q - lag, t)
-            if steps:
-                spread.step(steps.pop(0))
-        for q in range(total, total + 6):
-            for lag, t in ((6, 4), (5, 3), (4, 2), (3, 1)):
-                if 0 <= q - lag < total:
-                    fold(q - lag, t)
-            if steps:
-                spread.step(steps.pop(0))
-        for i in steps:
+
+        def chain():
+            for k, out in ((3, gpre4), (2, gpre3), (1, gpre2), (0, gpre1)):
+                waits = back(k, gact, out)
+                for at, _ in enumerate(waits):
+                    if (k, at) == (3, 1):
+                        groups = ggroup_ref.shape[0]
+                        member = (lax.broadcasted_iota(jnp.int32, (groups, rows), 0) == gid_ref[...]).astype(F32)
+                        gcell[...] = exact(member, ggroup_ref[...], ((0,), (0,)))
+                    if (k, at) == (1, 1):
+                        latent_side()
+                    yield 0
+                if k == 3:
+                    nrm_loads[1].start()
+                    gact[...] = nt(gpre4[...], d2_ref[...])
+                elif k == 2:
+                    nrm_loads[0].start()
+                    grad_z = nt(gpre3[...], d1_ref[...])
+                    mu = head_ref_in[:, 0:latent]
+                    logvar = head_ref_in[:, latent : 2 * latent]
+                    kl = KL_WEIGHT * genes / cell_total
+                    deviation = jnp.exp(0.5 * logvar)
+                    grad_mu = grad_z + kl * mu + gcell[:, 0:latent]
+                    grad_logvar = grad_z * noise_ref[...] * (0.5 * deviation) + 0.5 * kl * (jnp.exp(logvar) - 1.0)
+                    ghead[...] = jnp.concatenate([grad_mu, grad_logvar], axis=1).astype(BF16)
+                    gact[...] = nn(ghead[...], head_ref[...])
+                elif k == 1:
+                    gact[...] = nt(gpre2[...], w2_ref[...])
+                else:
+                    for copy in act_loads[:2]:
+                        copy.wait()
+                    xt_load.wait()
+                    waiting.extend(range(2 * STAGES + 1))
+                yield 0
+
+        waiting = []
+
+        def more():
+            if waiting and len(plan) % 12 == 0:
+                spread.step(waiting.pop(0))
+
+        run(chain(), more)
+        for i in waiting:
             spread.step(i)
         for q in (total - 2, total - 1):
             scatter.send(q, 0).wait_send()
@@ -1055,18 +1354,11 @@
             for k in range(4):
                 gather.finish(level, k)
 
-    last = genes - (genes * (PARTS - 1)) // PARTS // 128 * 128
-    pl.run_scoped(
-        finish,
-        pltpu.VMEM((PARTS, 224, rows), BF16),
-        pltpu.VMEM((3, rows, 384), BF16),
-        pltpu.VMEM((rows, last), BF16),
-        pltpu.VMEM((2, rows, hidden), BF16),
-    )
+    pl.run_scoped(finish, pltpu.VMEM(xt_hbm.shape, BF16), pltpu.VMEM((2, rows, hidden), BF16))
 
 
 def call_backward(grid, kept, cells_x, out_w, noise, gid, out_b, w2, headt, d1, d2, gain, shift):
-    (nrm0, nrm1, nrm2, nrm3, inv, act1, act2, zlat, act3, act4, head, ggroup) = kept
+    (nrm0, nrm1, nrm2, nrm3, inv, act1, act2, zlat, act3, act4, head, ggroup, xt) = kept
     rows, genes = cells_x.shape
     hidden, latent = w2.shape[0], d1.shape[0]
     spans = windows(genes)
@@ -1094,7 +1386,7 @@
         + [dma((4, size - 1)) for _, size in grid.digits]
         + [pltpu.VMEM((2, 16 * SLOT_ROWS, 128), F32), pltpu.VMEM((16 * SLOT_ROWS, 128), F32)]
         + [pltpu.VMEM((CHANNELS, (16 >> t) * SLOT_ROWS, 128), F32) for t in range(STAGES)]
-        + [dma((2,)), dma((CHANNELS, STAGES)), dma((CHANNELS, STAGES)), pltpu.SemaphoreType.REGULAR((CHANNELS, STAGES))]
+        + [dma((2,)), dma((CHANNELS, STAGES)), dma((CHANNELS, STAGES)), pltpu.SemaphoreType.REGULAR((2 * count + 2 - CHANNELS, STAGES))]
         + [pltpu.VMEM((REP_ROWS, 128), F32), pltpu.VMEM((REP_ROWS, 128), F32)]
         + [pltpu.VMEM((REP_ROWS >> (t + 1), 128), F32) for t in range(STAGES)]
         + [dma((4, STAGES))]
@@ -1111,12 +1403,12 @@
             pltpu.VMEM((2, rows, hidden), F32),
             pltpu.VMEM((SLOT_ROWS, 128), F32),
         ]
-        + [dma((2, count)), dma((count,)), dma((4,)), dma((PARTS,)), dma((3,))]
+        + [dma((2, count)), dma((count,)), dma((4,)), dma, dma((3,))]
     )
     return pl.pallas_call(
         functools.partial(backward_kernel, grid, latent),
         out_shape=out_shape,
-        in_specs=[hbm] * 9 + [vm] * 14,
+        in_specs=[hbm] * 10 + [vm] * 14,
         out_specs=[hbm] + [vm] * (len(out_shape) - 1),
         scratch_shapes=scratch,
         name="backward",
@@ -1133,6 +1425,7 @@
         act1,
         act2,
         act3,
+        xt,
         act4,
         zlat,
         head,

time: 523 us -> 369 us (0.71)
  Pallas kernels: 477 us -> 325 us
    pallas_call x1, Pallas kernels: 416 us -> 263 us  [call_backward(): pl.pallas_call(functools.partial(backward_kernel, grid, latent), out_shap...]
where the time goes in v3:
time: 369 us; the launch traced here: 363 us
  Pallas kernels  325 us (88%)
  local copies, waits for them, and re-layouts  19.2 us (5%)
  matrix products  17.8 us (5%)
    pallas_call x1, Pallas kernels, call_backward(): pl.pallas_call(functools.partial(backward_kernel, grid, latent), out_shap...  263 us
    pallas_call x1, Pallas kernels, call_forward(): pl.pallas_call(functools.partial(forward_kernel, grid), out_shape=out_sha...  61.8 us
    dot_general x1, matrix products, shards(): lax.dot_general(gpre1, enc_w1, (((1,), (1,)), ((), ())), preferred_elemen...  17.8 us
    unnamed x21, local copies, waits for them, and re-layouts  10.6 us

profile of v3, /device:TPU:0, one launch (start us, length us, event | category | flops | bytes accessed | tf_op | source)
XLA Modules:
  0.0 363.1 jit_solution(3554755526392843260)
XLA Ops:
  0.6 1.8 copy.28.noise_ref
  2.5 1.3 reshape.49.gid_ref
  3.7 1.4 copy.26.table_ref
  5.1 1.4 copy.27.mask_ref
  6.4 0.0 copy-start.4
  6.4 61.8 %forward.1 = (f32[576,800]{1,0:T(8,128)}, f32[576,800]{1,0:T(8,128)}, f32[576,800]{1,0:T(8,128)}, f32[576,800]{1,0:T(8,128)}, f32[4,800]{1,0:T(4,128)}, /*index=...) custom-call(s32[16,4]{1,0:T(8,128)} %copy.26.table_ref, ...), custom_call_target="tpu_custom_call" | custom-call | tf_op jit(solution)/shard_map/forward/pallas_call | solution.py:405
  68.3 0.0 copy-done.4
  68.3 0.6 reshape.51.outb_ref
  68.9 263.0 %backward.1 = (bf16[576,7168]{1,0:T(8,128)(2,1)}, bf16[576,800]{1,0:T(8,128)(2,1)}, f32[25,7168]{1,0:T(8,128)}, f32[224,800]{1,0:T(8,128)}, f32[56,800]{1,0:T(8,...) custom-call(bf16[576,7000]{1,0:T(8,128)(2,1)} %x_hbm.3, ...), custom_call_target="tpu_custom_call" | custom-call | tf_op jit(solution)/shard_map/backward/pallas_call | solution.py:1408
  331.9 0.0 copy-start.1
  331.9 0.0 copy-start
  331.9 0.0 copy-start.2
  331.9 0.0 copy-start.3
  331.9 0.0 copy-start.5
  331.9 17.8 %subtract_multiply_fusion = f32[576,7000]{1,0:T(8,128)} fusion(bf16[576,800]{1,0:T(8,128)(2,1)} %get-tuple-element.49, bf16[7000,800]{0,1:T(8,128)(2,1)} %param.20, bf16[576,7168]{1,0:T(8,128)(2,1)} %get-tuple-element.50), kind=kOutput, calls=%fused_computation | convolution fusion | flops 6463296000 | bytes 36313600 | tf_op jit(solution)/shard_map/dot_general | solution.py:1519
  349.8 0.0 copy-done.1
  349.8 0.6 reshape.52
  350.4 0.3 dynamic_slice.3
  350.7 1.5 reshape.53
  352.2 0.0 copy-done
  352.2 0.1 slice.18
  352.2 1.3 reshape.56
  353.5 1.8 reshape.54
  355.3 1.2 slice.17
  356.6 0.0 copy-done.2
  356.6 0.9 copy.36
  357.4 0.0 copy-done.3
  357.4 0.7 copy.37
  358.2 0.0 copy-done.5
  358.2 0.6 copy.38
  358.8 1.3 copy.39
  360.1 1.3 copy.40
  361.4 1.2 copy.41
Async XLA Ops:
  6.4 61.8 %copy-start.4 = (f32[7000]{0:T(1024)S(1)}, f32[7000]{0:T(1024)}, u32[]{:S(2)}) copy-start(f32[7000]{0:T(1024)} %param.27) | copy-start | bytes 84004
  331.9 17.9 %copy-start.1 = (f32[224,800]{1,0:T(8,128)S(1)}, f32[224,800]{1,0:T(8,128)}, u32[]{:S(2)}) copy-start(f32[224,800]{1,0:T(8,128)} %get-tuple-element.51) | copy-start | bytes 2150404
  331.9 20.2 %copy-start = (f32[25,7168]{1,0:T(8,128)S(1)}, f32[25,7168]{1,0:T(8,128)}, u32[]{:S(2)}) copy-start(f32[25,7168]{1,0:T(8,128)} %get-tuple-element.56) | copy-start | bytes 2150404
  331.9 24.7 %copy-start.2 = (f32[200,800]{1,0:T(8,128)S(1)}, f32[200,800]{1,0:T(8,128)}, u32[]{:S(2)}) copy-start(f32[200,800]{1,0:T(8,128)} %get-tuple-element.53) | copy-start | bytes 1920004
  331.9 25.5 %copy-start.3 = (f32[100,800]{1,0:T(8,128)S(1)}, f32[100,800]{1,0:T(8,128)}, u32[]{:S(2)}) copy-start(f32[100,800]{1,0:T(8,128)} %get-tuple-element.76) | copy-start | bytes 960004
  331.9 26.3 %copy-start.5 = (f32[56,128]{1,0:T(8,128)S(1)}, f32[56,128]{1,0:T(8,128)}, u32[]{:S(2)}) copy-start(f32[56,128]{1,0:T(8,128)} %get-tuple-element.57) | copy-start | bytes 86020
